TPU v7x, 32 devices: a whole 2x2x4 slice. The times are simulated.
32 devices in a mesh: row: 4 (over x, core), seq: 8 (over z, y).
Axes of the slice: x: 2, y: 2, z: 4, core: 2. Of those that a mesh axis runs over, the one named last changes fastest.
Arguments:
- tokens: bfloat16 [4, 4096, 768], P('row', 'seq'), may hold values from -6 to 6
- cotangent: bfloat16 [4, 4096, 768], P('row', 'seq'), may hold values from -6 to 6
- w_qkv: bfloat16 [768, 2304], replicated, may hold values from -0.21875 to 0.21875
- b_qkv: bfloat16 [2304], replicated, may hold values from -3 to 3
- w_out: bfloat16 [768, 768], replicated, may hold values from -4 to 4
- b_out: bfloat16 [768], replicated, may hold values from -3 to 3
- gain_one: float32 [768], replicated, may hold values from 0.1 to 1.9
- shift_one: float32 [768], replicated, may hold values from -3 to 3
- w_up: bfloat16 [768, 3072], P(None, 'seq'), may hold values from -0.21875 to 0.21875
- b_up: bfloat16 [3072], P('seq'), may hold values from -3 to 3
- w_down: bfloat16 [3072, 768], P('seq'), may hold values from -0.109375 to 0.109375
- b_down: bfloat16 [768], replicated, may hold values from -3 to 3
- gain_two: float32 [768], replicated, may hold values from 0.1 to 1.9
- shift_two: float32 [768], replicated, may hold values from -3 to 3
- feature_codes: int32 [12, 64, 64], replicated, may hold values from 0 to 15
- bias_table: float32 [12, 32], replicated, may hold values from -3 to 3
- offset_bucket: int32 [8191], replicated, may hold values from 0 to 31, as said below
Outputs:
- layer_out: bfloat16 [4, 4096, 768], P('row', 'seq')
- grad_tokens: float32 [4, 4096, 768], P('row', 'seq')
- grad_w_qkv: float32 [768, 2304], replicated
- grad_b_qkv: float32 [2304], replicated
- grad_w_out: float32 [768, 768], replicated
- grad_b_out: float32 [768], replicated
- grad_gain_one: float32 [768], replicated
- grad_shift_one: float32 [768], replicated
- grad_w_up: float32 [768, 3072], P(None, 'seq')
- grad_b_up: float32 [3072], P('seq')
- grad_w_down: float32 [3072, 768], P('seq')
- grad_b_down: float32 [768], replicated
- grad_gain_two: float32 [768], replicated
- grad_shift_two: float32 [768], replicated
- grad_bias_table: float32 [12, 32], replicated
Inputs may be any that keep to these rules, and one draw needn't show every extreme that they name: `offset_bucket`: entry j stands for the key offset j - (4095) from its query. Offsets below -128 all have bucket 32 - 2, offsets above 128 all have bucket 32 - 1, offset 0 has bucket 0, and every other offset has a bucket under 32 - 2.
All inputs are finite; a program needn't handle non-finite values.
Results may differ from a plain program's by a relative error of at most 0.025.
Values may be sent and summed in bfloat16 or wider, within the bound.
A program may use at most 384 MiB of HBM per device.

v0:
```python
import math

import jax
import jax.numpy as jnp
from jax import lax
from jax.sharding import PartitionSpec as P

WINDOW = 128


norm_eps = 1e-06
code_center = 7.5
code_spread = math.sqrt(21.25)
highest_precision_mode = lax.Precision.HIGHEST
root_half = 0.7071067811865476
inv_root_tau = 0.3989422804014327


def extended_2(block, sides, width):
    for axis, dim in sides:
        count = lax.axis_size(axis)
        forward = [(i, i + 1) for i in range(count - 1)]
        backward = [(target, source) for source, target in forward]
        low = lax.ppermute(
            lax.slice_in_dim(block, block.shape[dim] - width, None, axis=dim), axis, forward
        )
        high = lax.ppermute(lax.slice_in_dim(block, 0, width, axis=dim), axis, backward)
        block = jnp.concatenate([low, block, high], axis=dim)
    return block


def split_parts(values):
    upper = values.astype(jnp.bfloat16)
    lower = (values - upper.astype(jnp.float32)).astype(jnp.bfloat16)
    return (upper, lower)


def split_left(form, wide, narrow):
    upper, lower = split_parts(wide)
    return jnp.einsum(form, upper, narrow, preferred_element_type=jnp.float32) + jnp.einsum(
        form, lower, narrow, preferred_element_type=jnp.float32
    )


def divide_right_side(form, narrow, wide):
    upper, lower = split_parts(wide)
    return jnp.einsum(form, narrow, upper, preferred_element_type=jnp.float32) + jnp.einsum(
        form, narrow, lower, preferred_element_type=jnp.float32
    )


def divide_both_sides(form, first, second):
    first_up, first_low = split_parts(first)
    second_up, second_low = split_parts(second)
    return (
        jnp.einsum(form, first_up, second_up, preferred_element_type=jnp.float32)
        + jnp.einsum(form, first_up, second_low, preferred_element_type=jnp.float32)
        + jnp.einsum(form, first_low, second_up, preferred_element_type=jnp.float32)
    )


def layer_norm(values, gain_vec, shift_vec):
    center = values - jnp.mean(values, -1, keepdims=True)
    inv_scale = lax.rsqrt(jnp.mean(center * center, -1, keepdims=True) + norm_eps)
    normed = center * inv_scale
    return (normed * gain_vec + shift_vec, normed, inv_scale)


def norm_back(grad_out, normed, inv_scale, gain_vec):
    grad_normed = grad_out * gain_vec
    centered = grad_normed - jnp.mean(grad_normed, -1, keepdims=True)
    grad_in = inv_scale * (centered - normed * jnp.mean(grad_normed * normed, -1, keepdims=True))
    return (grad_in, jnp.sum(grad_out * normed, 0), jnp.sum(grad_out, 0))


def feature_map(rounded, omega_int):
    head_dim = rounded.shape[-1]
    factor = head_dim ** (-0.25) / code_spread
    widened = rounded.astype(jnp.float32)
    projected = (
        jnp.einsum("thd,hdm->thm", rounded, omega_int, preferred_element_type=jnp.float32) * factor
    )
    half_norm = jnp.sum(widened * widened, -1, keepdims=True) * (0.5 * head_dim ** (-0.5))
    return jnp.exp(projected - half_norm) * omega_int.shape[-1] ** (-0.5)


def feature_back(grad_feat, features, rounded, omega_int):
    head_dim = rounded.shape[-1]
    factor = head_dim ** (-0.25) / code_spread
    grad_inner = grad_feat * features
    grad_proj = split_left("thm,hdm->thd", grad_inner, omega_int) * factor
    return grad_proj - jnp.sum(grad_inner, -1, keepdims=True) * head_dim ** (-0.5) * rounded.astype(
        jnp.float32
    )


def toeplitz_rows(coef_vec, row_count, col_count):
    head_count, line_len = coef_vec.shape
    turned = jnp.roll(coef_vec, -(row_count - 1), axis=-1)
    flat_line = jnp.tile(turned, (1, row_count))[:, : row_count * (line_len - 1)]
    return flat_line.reshape(head_count, row_count, line_len - 1)[:, :, :col_count]


def toeplitz_sums(band_block, line_len):
    head_count, row_count, col_count = band_block.shape
    padded = jnp.pad(band_block, ((0, 0), (0, 0), (0, line_len - 1 - col_count)))
    flat_line = jnp.pad(
        padded.reshape(head_count, row_count * (line_len - 1)), ((0, 0), (0, row_count))
    )
    folded = jnp.sum(flat_line.reshape(head_count, row_count, line_len), 1)
    return jnp.roll(folded, row_count - 1, axis=-1)


def gelu_slope(values):
    return 0.5 * (1.0 + lax.erf(values * root_half)) + values * inv_root_tau * jnp.exp(
        -0.5 * values * values
    )


def key_sums(key_portion, value_portion):
    return (
        jnp.einsum("qge,qgs->ges", key_portion, value_portion, preferred_element_type=jnp.float32),
        jnp.sum(key_portion.astype(jnp.float32), 0),
    )


def row_grads(key_portion, value_portion, key_value_gradient, key_gradient):
    gradient_key_rows = (
        divide_right_side("zyo,yro->zyr", value_portion, key_value_gradient) + key_gradient[None]
    )
    gradient_value_rows = divide_right_side("oyx,yxs->oys", key_portion, key_value_gradient)
    return (gradient_key_rows, gradient_value_rows)


def shards(
    tokens,
    cotangent,
    w_qkv,
    b_qkv,
    w_out,
    b_out,
    gain_one,
    shift_one,
    w_up,
    b_up,
    w_down,
    b_down,
    gain_two,
    shift_two,
    feature_codes,
    bias_table,
    offset_bucket,
):
    seq_rows = tokens.shape[1]
    model_width = tokens.shape[2]
    head_count, head_dim, feat_count = feature_codes.shape
    bucket_count = bias_table.shape[1]
    window_len = WINDOW
    ext_len = seq_rows + 2 * window_len
    line_len = 2 * seq_rows + 2 * window_len - 1
    total_len = (offset_bucket.shape[0] + 1) // 2
    feat_width = head_count * feat_count
    omega_int = (feature_codes.astype(jnp.float32) - code_center).astype(jnp.bfloat16)
    local_in = tokens[0]
    qkv_proj = jnp.dot(local_in, w_qkv, preferred_element_type=jnp.float32) + b_qkv.astype(
        jnp.float32
    )
    q_low = qkv_proj[:, :model_width].astype(jnp.bfloat16).reshape(seq_rows, head_count, head_dim)
    k_low = (
        qkv_proj[:, model_width : 2 * model_width]
        .astype(jnp.bfloat16)
        .reshape(seq_rows, head_count, head_dim)
    )
    v_low = (
        qkv_proj[:, 2 * model_width :].astype(jnp.bfloat16).reshape(seq_rows, head_count, head_dim)
    )
    q_phi = feature_map(q_low, omega_int)
    k_phi = feature_map(k_low, omega_int)
    query_features = q_phi.astype(jnp.bfloat16)
    k_feat = k_phi.astype(jnp.bfloat16)
    joined = jnp.concatenate(
        [k_feat.reshape(seq_rows, feat_width), v_low.reshape(seq_rows, model_width)], 1
    )
    extended = extended_2(joined, (("seq", 0),), window_len)
    k_ext = extended[:, :feat_width].reshape(ext_len, head_count, feat_count)
    v_ext = extended[:, feat_width:].reshape(ext_len, head_count, head_dim)
    line_start = total_len - seq_rows - window_len
    bucket_line = offset_bucket[line_start : line_start + line_len]
    one_hot = (bucket_line[:, None] == jnp.arange(bucket_count, dtype=jnp.int32)[None, :]).astype(
        jnp.float32
    )
    coef_line = jnp.exp(
        jnp.dot(bias_table, jnp.transpose(one_hot), precision=highest_precision_mode)
    )
    coef_band = toeplitz_rows(coef_line, seq_rows, ext_len)
    scores = jnp.einsum("thm,ehm->hte", query_features, k_ext, preferred_element_type=jnp.float32)
    weights = coef_band * scores
    numerator_window = split_left("hte,ehd->thd", weights, v_ext)
    denom_band = jnp.transpose(jnp.sum(weights, -1))
    own_kv, own_k = key_sums(k_feat, v_low)
    left_kv, left_k = key_sums(k_ext[:window_len], v_ext[:window_len])
    right_kv, right_k = key_sums(k_ext[seq_rows + window_len :], v_ext[seq_rows + window_len :])
    block_key_value, block_k = (
        lax.all_gather(own_kv[None], "seq", axis=0, tiled=True),
        lax.all_gather(own_k[None], "seq", axis=0, tiled=True),
    )
    shard_ids = jnp.arange(lax.axis_size("seq"), dtype=jnp.int32)
    my_index = lax.axis_index("seq")
    leading_mask = (shard_ids < my_index).astype(jnp.float32)
    running_key_value = jnp.einsum(
        "r,rucs->ucs", leading_mask, block_key_value, precision=highest_precision_mode
    )
    prefix_k = jnp.einsum("n,nhm->hm", leading_mask, block_k, precision=highest_precision_mode)
    far_left_kv = running_key_value - left_kv
    far_left_k = prefix_k - left_k
    far_right_kv = jnp.sum(block_key_value, 0) - running_key_value - own_kv - right_kv
    far_right_k = jnp.sum(block_k, 0) - prefix_k - own_k - right_k
    left_coef = jnp.exp(bias_table[:, bucket_count - 2])
    right_coef = jnp.exp(bias_table[:, bucket_count - 1])
    blended_key_value = (
        left_coef[:, None, None] * far_left_kv + right_coef[:, None, None] * far_right_kv
    )
    mixed_k = left_coef[:, None] * far_left_k + right_coef[:, None] * far_right_k
    attention_numerator = numerator_window + divide_right_side(
        "oyx,yxs->oys", query_features, blended_key_value
    )
    denominator = denom_band + divide_right_side("thm,hm->th", query_features, mixed_k)
    attn_out = attention_numerator / denominator[:, :, None]
    attn_low = attn_out.reshape(seq_rows, model_width).astype(jnp.bfloat16)
    first_sum = (
        local_in.astype(jnp.float32)
        + jnp.dot(attn_low, w_out, preferred_element_type=jnp.float32)
        + b_out.astype(jnp.float32)
    )
    hidden_one, normed_one, scale_one = layer_norm(first_sum, gain_one, shift_one)
    hidden_low = hidden_one.astype(jnp.bfloat16)
    gathered = lax.all_gather(hidden_low, "seq", axis=0, tiled=True)
    pre_up = jnp.dot(gathered, w_up, preferred_element_type=jnp.float32) + b_up.astype(jnp.float32)
    act_low = jax.nn.gelu(pre_up, approximate=False).astype(jnp.bfloat16)
    ffn_out = lax.psum_scatter(
        jnp.dot(act_low, w_down, preferred_element_type=jnp.float32).astype(jnp.bfloat16),
        "seq",
        scatter_dimension=0,
        tiled=True,
    ).astype(jnp.float32)
    second_sum = hidden_one + ffn_out + b_down.astype(jnp.float32)
    layer_out, normed_two, scale_two = layer_norm(second_sum, gain_two, shift_two)
    grad_out = cotangent[0].astype(jnp.float32)
    grad_second, grad_gain_two, grad_shift_two = norm_back(
        grad_out, normed_two, scale_two, gain_two
    )
    grad_ffn_low = grad_second.astype(jnp.bfloat16)
    grad_b_down = jnp.sum(grad_ffn_low.astype(jnp.float32), 0)
    grad_rows = lax.all_gather(grad_ffn_low, "seq", axis=0, tiled=True)
    grad_act = jnp.einsum("rd,fd->rf", grad_rows, w_down, preferred_element_type=jnp.float32)
    grad_pre_low = (grad_act * gelu_slope(pre_up)).astype(jnp.bfloat16)
    grad_hidden = grad_second + lax.psum_scatter(
        jnp.einsum("rf,df->rd", grad_pre_low, w_up, preferred_element_type=jnp.float32).astype(
            jnp.bfloat16
        ),
        "seq",
        scatter_dimension=0,
        tiled=True,
    ).astype(jnp.float32)
    part_up = jnp.einsum("rd,rf->df", gathered, grad_pre_low, preferred_element_type=jnp.float32)
    part_bias = jnp.sum(grad_pre_low.astype(jnp.float32), 0)
    part_down = jnp.einsum("rf,rd->fd", act_low, grad_rows, preferred_element_type=jnp.float32)
    grad_w_up, grad_b_up, grad_w_down = (
        lax.psum(part_up.astype(jnp.bfloat16), "row").astype(jnp.float32),
        lax.psum(part_bias.astype(jnp.bfloat16), "row").astype(jnp.float32),
        lax.psum(part_down.astype(jnp.bfloat16), "row").astype(jnp.float32),
    )
    grad_first, grad_gain_one, grad_shift_one = norm_back(
        grad_hidden, normed_one, scale_one, gain_one
    )
    grad_z_low = grad_first.astype(jnp.bfloat16)
    grad_b_out = jnp.sum(grad_z_low.astype(jnp.float32), 0)
    grad_w_out = jnp.einsum("ra,rb->ab", attn_low, grad_z_low, preferred_element_type=jnp.float32)
    grad_attn = jnp.einsum(
        "rb,ab->ra", grad_z_low, w_out, preferred_element_type=jnp.float32
    ).reshape(seq_rows, head_count, head_dim)
    numerator_gradient = grad_attn / denominator[:, :, None]
    grad_denom = -jnp.sum(grad_attn * attn_out, -1) / denominator
    grad_weights = (
        split_left("thd,ehd->hte", numerator_gradient, v_ext)
        + jnp.transpose(grad_denom)[:, :, None]
    )
    grad_v_ext = divide_both_sides("hte,thd->ehd", weights, numerator_gradient)
    grad_scores = coef_band * grad_weights
    grad_q_feat = split_left("hte,ehm->thm", grad_scores, k_ext)
    grad_k_ext = split_left("hte,thm->ehm", grad_scores, query_features)
    grad_line = toeplitz_sums(grad_weights * weights, line_len)
    grad_table = jnp.dot(grad_line, one_hot, precision=highest_precision_mode)
    blended_key_value_gradient = divide_right_side(
        "qge,qgs->ges", query_features, numerator_gradient
    )
    grad_mixed_k = divide_right_side("thm,th->hm", query_features, grad_denom)
    grad_q_feat = (
        grad_q_feat
        + divide_both_sides("zyo,yro->zyr", numerator_gradient, blended_key_value)
        + grad_denom[:, :, None] * mixed_k[None]
    )
    left_grad = left_coef * (
        jnp.sum(blended_key_value_gradient * far_left_kv, (1, 2))
        + jnp.sum(grad_mixed_k * far_left_k, 1)
    )
    right_grad = right_coef * (
        jnp.sum(blended_key_value_gradient * far_right_kv, (1, 2))
        + jnp.sum(grad_mixed_k * far_right_k, 1)
    )
    grad_table = (
        grad_table.at[:, bucket_count - 2].add(left_grad).at[:, bucket_count - 1].add(right_grad)
    )
    grad_left_kv = left_coef[:, None, None] * blended_key_value_gradient
    grad_left_k = left_coef[:, None] * grad_mixed_k
    grad_right_kv = right_coef[:, None, None] * blended_key_value_gradient
    grad_right_k = right_coef[:, None] * grad_mixed_k
    block_group_key_value, block_gp_k, block_gr_kv, block_gr_k = (
        lax.all_gather((grad_left_kv - grad_right_kv)[None], "seq", axis=0, tiled=True),
        lax.all_gather((grad_left_k - grad_right_k)[None], "seq", axis=0, tiled=True),
        lax.all_gather(grad_right_kv[None], "seq", axis=0, tiled=True),
        lax.all_gather(grad_right_k[None], "seq", axis=0, tiled=True),
    )
    trailing_mask = (shard_ids > my_index).astype(jnp.float32)
    grad_own_kv = (
        jnp.einsum(
            "r,rucs->ucs", trailing_mask, block_group_key_value, precision=highest_precision_mode
        )
        + jnp.sum(block_gr_kv, 0)
        - grad_right_kv
    )
    grad_own_k = (
        jnp.einsum("n,nhm->hm", trailing_mask, block_gp_k, precision=highest_precision_mode)
        + jnp.sum(block_gr_k, 0)
        - grad_right_k
    )
    left_k_add, left_v_add = row_grads(
        k_ext[:window_len], v_ext[:window_len], -grad_left_kv, -grad_left_k
    )
    own_k_add, own_v_add = row_grads(k_feat, v_low, grad_own_kv, grad_own_k)
    right_k_add, right_v_add = row_grads(
        k_ext[seq_rows + window_len :],
        v_ext[seq_rows + window_len :],
        -grad_right_kv,
        -grad_right_k,
    )
    grad_k_ext = grad_k_ext + jnp.concatenate([left_k_add, own_k_add, right_k_add], 0)
    grad_v_ext = grad_v_ext + jnp.concatenate([left_v_add, own_v_add, right_v_add], 0)
    packed = jnp.concatenate(
        [grad_k_ext.reshape(ext_len, feat_width), grad_v_ext.reshape(ext_len, model_width)], 1
    )
    outgoing = jnp.concatenate([packed[:window_len], packed[seq_rows + window_len :]], 0)
    incoming = extended_2(outgoing.astype(jnp.bfloat16), (("seq", 0),), window_len).astype(
        outgoing.dtype
    )
    own_grad = packed[window_len : window_len + seq_rows]
    own_grad = own_grad.at[:window_len].add(incoming[:window_len])
    own_grad = own_grad.at[seq_rows - window_len :].add(incoming[3 * window_len :])
    grad_k_feat = own_grad[:, :feat_width].reshape(seq_rows, head_count, feat_count)
    grad_v = own_grad[:, feat_width:]
    grad_q = feature_back(grad_q_feat, q_phi, q_low, omega_int)
    key_gradient = feature_back(grad_k_feat, k_phi, k_low, omega_int)
    grad_qkv_low = jnp.concatenate(
        [
            grad_q.reshape(seq_rows, model_width),
            key_gradient.reshape(seq_rows, model_width),
            grad_v,
        ],
        1,
    ).astype(jnp.bfloat16)
    grad_b_qkv = jnp.sum(grad_qkv_low.astype(jnp.float32), 0)
    grad_w_qkv = jnp.einsum("rd,re->de", local_in, grad_qkv_low, preferred_element_type=jnp.float32)
    grad_tokens = grad_first + jnp.einsum(
        "re,de->rd", grad_qkv_low, w_qkv, preferred_element_type=jnp.float32
    )
    summed = lax.psum(
        (
            grad_w_qkv,
            grad_b_qkv,
            grad_w_out,
            grad_b_out,
            grad_gain_one,
            grad_shift_one,
            grad_b_down,
            grad_gain_two,
            grad_shift_two,
            grad_table,
        ),
        ("row", "seq"),
    )
    return (
        layer_out.astype(jnp.bfloat16)[None],
        grad_tokens[None],
        summed[0],
        summed[1],
        summed[2],
        summed[3],
        summed[4],
        summed[5],
        grad_w_up,
        grad_b_up,
        grad_w_down,
        summed[6],
        summed[7],
        summed[8],
        summed[9],
    )


def solution(mesh):
    placed = (
        P("row", "seq", None),
        P("row", "seq", None),
        P(),
        P(),
        P(),
        P(),
        P(),
        P(),
        P(None, "seq"),
        P("seq"),
        P("seq", None),
        P(),
        P(),
        P(),
        P(),
        P(),
        P(),
    )
    return jax.shard_map(
        shards,
        mesh=mesh,
        in_specs=placed,
        out_specs=(
            P("row", "seq", None),
            P("row", "seq", None),
            P(),
            P(),
            P(),
            P(),
            P(),
            P(),
            P(None, "seq"),
            P("seq"),
            P("seq", None),
            P(),
            P(),
            P(),
            P(),
        ),
        check_vma=False,
    )
```

profile of v0, /device:TPU:0, one launch (start us, length us, event | category | flops | bytes accessed | tf_op | source)
XLA Modules:
  0.0 1373.6 jit_solution(11363240409369681656)
XLA Ops:
  46.4 36.9 %all-gather.6 = f32[8,12,64]{2,1,0:T(8,128)S(1)} all-gather(f32[1,12,64]{2,1,0:T(8,128)S(1)} %bitcast.302), channel_id=3, replica_groups=mesh['row'=4,'seq'=8] {'seq'}, dimensions={0}, use_global_device_ids=true | all-gather | bytes 27648 | tf_op jit(solution)/shard_map/all_gather | solution.py:205
  86.9 10.5 tile.4
  97.4 47.8 %tile.10 = f32[12,654848]{1,0:T(8,128)} reshape(f32[12,512,1279]{2,1,0:T(8,128)} %tile.4) | data formatting | bytes 62865408 | tf_op jit(solution)/shard_map/tile | solution.py:100
  145.3 28.4 %slice.230 = f32[12,654336]{1,0:T(8,128)} slice(f32[12,654848]{1,0:T(8,128)} %tile.10), slice={[0:12], [0:654336]} | slice | bytes 62816256 | tf_op jit(solution)/shard_map/slice | solution.py:100
  173.7 89.8 %reshape.289 = f32[12,512,1278]{2,1,0:T(8,128)} reshape(f32[12,654336]{1,0:T(8,128)} %slice.230) | data formatting | bytes 62816256 | tf_op jit(solution)/shard_map/reshape | solution.py:101
  295.5 16.1 %fusion.153 = (f32[12,512]{1,0:T(8,128)S(1)}, f32[12,512,768]{2,1,0:T(8,128)}) fusion(bf16[512,12,64]{0,2,1:T(8,128)(2,1)} %get-tuple-element.175, bf16[768,12,64]{0,2,1:T(8,128)(2,1)} %bitcast.262, f32[12,512,1278]{2,1,0:T(8,128)} %reshape.289), kind=kOutput, calls=%fused_computation.284 | convolution fusion | flops 613410816 | bytes 39739392 | tf_op jit(solution)/shard_map/thm,ehm->hte/dot_general | solution.py:196
  312.9 15.9 %fusion.134 = f32[12,64,512]{2,1,0:T(8,128)} fusion(bf16[768,12,64]{0,2,1:T(8,128)(2,1)S(1)} %bitcast.254, f32[12,512,768]{2,1,0:T(8,128)} %get-tuple-element.181), kind=kOutput, calls=%fused_computation.269 | convolution fusion | flops 622854144 | bytes 21626880 | tf_op jit(solution)/shard_map/hte,ehd->thd/dot_general | solution.py:40
  339.9 11.5 fusion.154
  357.8 95.1 %all-gather.15.cloned.1.call-done = bf16[4096,768]{1,0:T(8,128)(2,1)} async-done(((bf16[512,768]{1,0:T(8,128)(2,1)}), bf16[4096,768]{1,0:T(8,128)(2,1)}) %all-gather.15.cloned.1.call-update) | async-done | bytes 6291472 | tf_op jit(solution)/shard_map/all_gather | solution.py:237
  452.8 19.0 %fusion.3 = (bf16[4096,384]{1,0:T(8,128)(2,1)S(1)}, f32[4096,384]{1,0:T(8,128)}) fusion(f32[384]{0:T(512)} %convert_element_type.279, bf16[4096,768]{1,0:T(8,128)(2,1)} %all-gather.15.cloned.1.call-done, bf16[768,384]{1,0:T(8,128)(2,1)} %param.33), kind=kOutput, calls=%fused_computation.17 | convolution fusion | flops 2519728128 | bytes 16320000 | tf_op jit(solution)/shard_map/dot_general | solution.py:238
  480.2 115.0 %reduce-scatter.3.cloned.1.call-done = bf16[512,768]{1,0:T(8,128)(2,1)} async-done(((bf16[4096,768]{1,0:T(8,128)(2,1)}), bf16[512,768]{1,0:T(8,128)(2,1)}) %reduce-scatter.3.cloned.1.call-update) | async-done | bytes 786448 | tf_op jit(solution)/shard_map/reduce_scatter | solution.py:240
  602.2 98.3 %all-gather.17.cloned.1.call-done = bf16[4096,768]{1,0:T(8,128)(2,1)} async-done(((bf16[512,768]{1,0:T(8,128)(2,1)}), bf16[4096,768]{1,0:T(8,128)(2,1)}) %all-gather.17.cloned.1.call-update) | async-done | bytes 6291472 | tf_op jit(solution)/shard_map/all_gather | solution.py:254
  700.4 9.5 fusion.157
  717.1 116.2 %reduce-scatter.5.cloned.1.call-done = bf16[512,768]{1,0:T(8,128)(2,1)} async-done(((bf16[4096,768]{1,0:T(8,128)(2,1)}), bf16[512,768]{1,0:T(8,128)(2,1)}) %reduce-scatter.5.cloned.1.call-update) | async-done | bytes 786448 | tf_op jit(solution)/shard_map/reduce_scatter | solution.py:257
  843.9 7.3 convolution_convert_fusion.2
  851.3 6.4 convolution_convert_fusion.3
  871.3 10.2 fusion.136
  881.4 9.8 fusion.138
  891.2 7.8 fusion.159
  901.1 30.6 %all-gather.7 = f32[8,12,64]{2,1,0:T(8,128)S(1)} all-gather(f32[1,12,64]{2,1,0:T(8,128)S(1)} %get-tuple-element.172), channel_id=6, replica_groups=mesh['row'=4,'seq'=8] {'seq'}, dimensions={0}, use_global_device_ids=true | all-gather | bytes 27648 | tf_op jit(solution)/shard_map/all_gather | solution.py:320
  932.4 32.8 %all-gather.8 = f32[8,12,64]{2,1,0:T(8,128)} all-gather(f32[1,12,64]{2,1,0:T(8,128)S(1)} %get-tuple-element.174), channel_id=7, replica_groups=mesh['row'=4,'seq'=8] {'seq'}, dimensions={0}, use_global_device_ids=true | all-gather | bytes 27648 | tf_op jit(solution)/shard_map/all_gather | solution.py:322
  971.5 32.9 %subtract_convert_fusion = (bf16[12,512,768]{2,1,0:T(8,128)(2,1)}, bf16[12,512,768]{2,1,0:T(8,128)(2,1)}, f32[12,512,768]{2,1,0:T(8,128)}) fusion(f32[12,512,1278]{2,1,0:T(8,128)} %reshape.289, f32[12,512,768]{2,1,0:T(8,128)} %get-tuple-element.181, f32[12,512]{1,0:T(8,128)S(1)} %copy-done.78, f32[12,512,768]{2,1,0:T(8,128)} %fusion.159, ...), kind=kOutput, calls=%fused_computation | convolution fusion | flops 641728512 | bytes 96362496 | tf_op jit(solution)/shard_map/thd,ehd->hte/dot_general | solution.py:40
  1004.4 8.0 fusion.160
  1015.5 6.4 fusion.156
  1045.5 13.0 maximum_add_fusion.1
  1093.9 19.1 %pad.16 = f32[12,512,1278]{2,1,0:T(8,128)} pad(f32[12,512,768]{2,1,0:T(8,128)} %get-tuple-element.152, f32[]{:T(128)} %constant.164.clone.1), padding=0_0x0_0x0_510 | pad | bytes 50282500 | tf_op jit(solution)/shard_map/jit(_pad)/pad | solution.py:106
  1113.1 59.1 %reshape.299 = f32[12,654336]{1,0:T(8,128)} reshape(f32[12,512,1278]{2,1,0:T(8,128)} %pad.16) | data formatting | bytes 62816256 | tf_op jit(solution)/shard_map/reshape | solution.py:108
  1172.2 28.3 %pad.17 = f32[12,654848]{1,0:T(8,128)} pad(f32[12,654336]{1,0:T(8,128)} %reshape.299, f32[]{:T(128)} %constant.164.clone.1), padding=0_0x0_512 | pad | bytes 62840836 | tf_op jit(solution)/shard_map/jit(_pad)/pad | solution.py:107
  1200.5 81.4 %reshape.300 = f32[12,512,1279]{2,1,0:T(8,128)} reshape(f32[12,654848]{1,0:T(8,128)} %pad.17) | data formatting | bytes 62865408 | tf_op jit(solution)/shard_map/reshape | solution.py:110
  1281.9 11.8 reduce_sum.344
  1309.0 41.2 %all-reduce.2 = (f32[2304]{0:T(1024)}, f32[768]{0:T(1024)}, f32[768]{0:T(1024)}, f32[768]{0:T(1024)}, f32[768]{0:T(1024)}, /*index=5*/f32[768]{0:T(1024)}, f32[768]{0:T(1024)}, f32[12,32]{1,0:T(8,128)}) all-reduce(f32[2304]{0:T(1024)} %convert_reduce_fusion, ...), channel_id=1, replica_groups=mesh['row'=4,'seq'=8] {'row','seq'}, use_global_device_ids=true, to_apply=%region_25.26 | all-reduce | flops 7296 | bytes 58368 | tf_op jit(solution)/shard_map/psum | solution.py:376
  1355.5 8.0 copy.120
  (397 shorter events, 234.1 us)
Async XLA Ops:
  7.2 321.6 %all-gather.19.cloned.1.call-start = ((), (), s32[]{:S(2)}) async-start(), calls=%async_computation.6 | async-start | bytes 3538944 | tf_op jit(solution)/shard_map/all_gather | solution.py:204
  26.2 12.7 copy-start.79
  26.2 426.6 %all-gather.15.cloned.1.call-start = ((), (), s32[]{:S(2)}) async-start(), calls=%async_computation.2 | async-start | bytes 7077888 | tf_op jit(solution)/shard_map/all_gather | solution.py:237
  30.7 236.7 %collective-permute-start = (bf16[128,1536]{1,0:T(8,128)(2,1)}, bf16[128,1536]{1,0:T(8,128)(2,1)}, u32[]{:S(2)}, u32[]{:S(2)}) collective-permute-start(bf16[128,1536]{1,0:T(8,128)(2,1)} %get-tuple-element.162), channel_id=1, source_target_pairs={{0,1},{1,2},{2,3},{3,4},{4,5},{5,6},{6,7},{8,9},{9,10},{10,11},{11... | collective-permute-start | bytes 1179656 | tf_op jit(solution)/shard_map/ppermute | solution.py:24
  36.3 233.4 %collective-permute-start.1 = (bf16[128,1536]{1,0:T(8,128)(2,1)}, bf16[128,1536]{1,0:T(8,128)(2,1)}, u32[]{:S(2)}, u32[]{:S(2)}) collective-permute-start(bf16[128,1536]{1,0:T(8,128)(2,1)} %get-tuple-element.163), channel_id=1, source_target_pairs={{1,0},{2,1},{3,2},{4,3},{5,4},{6,5},{7,6},{9,8},{10,9},{11,10},{12... | collective-permute-start | bytes 1179656 | tf_op jit(solution)/shard_map/ppermute | solution.py:27
  295.5 16.1 %copy-start.77 = (f32[12,1,512]{2,1,0:T(1,128)}, f32[12,1,512]{2,1,0:T(1,128)S(1)}, u32[]{:S(2)}) copy-start(f32[12,1,512]{2,1,0:T(1,128)S(1)} %fusion.90) | copy-start | bytes 73732
  295.5 16.8 %copy-start.76 = (f32[12,1,512]{2,1,0:T(1,128)S(1)}, f32[12,1,512]{2,1,0:T(1,128)}, u32[]{:S(2)}) copy-start(f32[12,1,512]{2,1,0:T(1,128)} %fusion.88) | copy-start | bytes 73732
  295.5 17.4 %copy-start.16 = (bf16[768,768]{0,1:T(8,128)(2,1)S(1)}, bf16[768,768]{0,1:T(8,128)(2,1)}, u32[]{:S(2)}) copy-start(bf16[768,768]{0,1:T(8,128)(2,1)} %copy.100) | copy-start | bytes 3538948
  339.9 11.5 copy-start.106
  356.5 238.7 %reduce-scatter.3.cloned.1.call-start = ((), (), s32[]{:S(2)}) async-start(), calls=%async_computation.3 | async-start | bytes 7077888 | tf_op jit(solution)/shard_map/reduce_scatter | solution.py:240
  452.8 20.7 %copy-start.109 = (bf16[384,768]{1,0:T(8,128)(2,1)S(1)}, bf16[384,768]{1,0:T(8,128)(2,1)}, u32[]{:S(2)}) copy-start(bf16[384,768]{1,0:T(8,128)(2,1)} %param.35) | copy-start | bytes 1769476
  478.8 221.6 %all-gather.17.cloned.1.call-start = ((), (), s32[]{:S(2)}) async-start(), calls=%async_computation.4 | async-start | bytes 7077888 | tf_op jit(solution)/shard_map/all_gather | solution.py:254
  602.1 231.2 %reduce-scatter.5.cloned.1.call-start = ((), (), s32[]{:S(2)}) async-start(), calls=%async_computation.5 | async-start | bytes 7077888 | tf_op jit(solution)/shard_map/reduce_scatter | solution.py:257
  700.4 11.2 copy-start.110
  717.0 309.8 %all-gather.23.cloned.1.call-start = ((), (), s32[]{:S(2)}) async-start(), calls=%async_computation.8 | async-start | bytes 3538944 | tf_op jit(solution)/shard_map/all_gather | solution.py:321
  843.1 186.7 %all-gather.21.cloned.1.call-start = ((), (), s32[]{:S(2)}) async-start(), calls=%async_computation.7 | async-start | bytes 3538944 | tf_op jit(solution)/shard_map/all_gather | solution.py:319
  843.9 245.7 %all-reduce.10.cloned.1.call-start = ((), (), s32[]{:S(2)}) async-start(), calls=%async_computation.10 | async-start | bytes 2359296 | tf_op jit(solution)/shard_map/psum | solution.py:269
  857.7 497.8 %all-reduce.8.cloned.1.call-start = ((), (), s32[]{:S(2)}) async-start(), calls=%async_computation.9 | async-start | bytes 18874368 | tf_op jit(solution)/shard_map/psum | solution.py:376
  858.0 8.7 copy-start.23
  858.0 8.7 copy-start.32
  860.4 39.0 %copy-start.73 = (f32[512,12]{0,1:T(8,128)}, f32[512,12]{0,1:T(8,128)S(1)}, u32[]{:S(2)}) copy-start(f32[512,12]{0,1:T(8,128)S(1)} %get-tuple-element.142) | copy-start | bytes 73732
  881.4 9.8 copy-start.18
  891.2 8.5 copy-start.84
  891.2 8.5 copy-start.89
  891.2 8.5 copy-start.97
  891.2 9.2 copy-start.87
  971.5 32.9 %copy-start.27 = (bf16[768,768]{0,1:T(8,128)(2,1)S(1)}, bf16[768,768]{0,1:T(8,128)(2,1)}, u32[]{:S(2)}) copy-start(bf16[768,768]{0,1:T(8,128)(2,1)} %copy.103) | copy-start | bytes 3538948
  1004.4 8.0 copy-start.1
  1004.4 8.0 copy-start.6
  1058.9 11.8 collective-permute-start.2
  1061.2 9.7 collective-permute-start.3
  1281.9 19.6 %copy-start.80 = (f32[12,32]{1,0:T(8,128)S(1)}, f32[12,32]{1,0:T(8,128)}, u32[]{:S(2)}) copy-start(f32[12,32]{1,0:T(8,128)} %param.40) | copy-start | bytes 4612
  (94 other events, 297.8 us)
Sparse Core Ops, SparseCore 0:
  26.4 73.7 all-gather.18
  356.6 96.2 all-gather.14
  479.0 116.1 reduce-scatter.2
  602.2 98.1 all-gather.16
  717.1 116.1 reduce-scatter.4
  843.3 59.5 all-gather.22
  905.1 60.0 all-gather.20
  967.5 36.3 all-reduce.9
  1081.0 191.6 all-reduce.7
where the time goes:
time: 1380 us; the launch traced here: 1370 us
  waiting for transfers between devices  431 us (31%)
  local copies, waits for them, and re-layouts  429 us (31%)
  matrix products  262 us (19%)
  blocking collectives  147 us (11%)
  other arithmetic  77.6 us (6%)
  between operations  15.3 us (1%)
    reduce_scatter x1, waiting for transfers between devices, shards(): lax.psum_scatter(jnp.einsum('rf,df->rd', grad_pre_low, w_up, preferred_el...  116 us
    reduce_scatter x1, waiting for transfers between devices, shards(): lax.psum_scatter(jnp.dot(act_low, w_down, preferred_element_type=jnp.floa...  115 us
    all_gather x1, waiting for transfers between devices, shards(): grad_rows = lax.all_gather(grad_ffn_low, 'seq', axis=0, tiled=True)  98.3 us
    all_gather x1, waiting for transfers between devices, shards(): gathered = lax.all_gather(hidden_low, 'seq', axis=0, tiled=True)  95.1 us
    reshape x1, local copies, waits for them, and re-layouts, toeplitz_rows(): flat_line.reshape(head_count, row_count, line_len - 1)[:, :, :col_count]  89.8 us
    reshape x1, local copies, waits for them, and re-layouts, toeplitz_sums(): folded = jnp.sum(flat_line.reshape(head_count, row_count, line_len), 1)  81.4 us
    dot_general x6, matrix products, split_left(): jnp.einsum(form, lower, narrow, preferred_element_type=jnp.float32)  64.7 us
    reshape x1, local copies, waits for them, and re-layouts, toeplitz_sums(): padded.reshape(head_count, row_count * (line_len - 1))  59.1 us
  transfers between devices with their start and end apart: 13, of which 6 were waited for; matrix products, arithmetic and copies ran while one was open for 47% of the time, Pallas kernels for 0%

commit v1 on v0

v1 whole, which is shorter than its diff:
```python
import functools
import math

import jax
import jax.numpy as jnp
from jax import lax
from jax.experimental import pallas as pl
from jax.experimental.pallas import tpu as pltpu
from jax.sharding import PartitionSpec as P

WINDOW = 128
LANES = 128
LINE = 512
CHUNK = 256
EPS = 1e-06
CENTER = 7.5
SPREAD = math.sqrt(21.25)
ROOT_HALF = 0.7071067811865476
INV_ROOT_TAU = 0.3989422804014327
MIB = 1 << 20
F32 = jnp.float32
BF16 = jnp.bfloat16


def nn(a, b):
    return lax.dot_general(a, b, (((1,), (0,)), ((), ())), preferred_element_type=F32)


def nt(a, b):
    return lax.dot_general(a, b, (((1,), (1,)), ((), ())), preferred_element_type=F32)


def tn(a, b):
    return lax.dot_general(a, b, (((0,), (0,)), ((), ())), preferred_element_type=F32)


def halves(values):
    upper = values.astype(BF16)
    return upper, (values - upper.astype(F32)).astype(BF16)


def block_ones(size, head_dim):
    rows = lax.broadcasted_iota(jnp.int32, (size, size), 0) // head_dim
    cols = lax.broadcasted_iota(jnp.int32, (size, size), 1) // head_dim
    return jnp.where(rows == cols, 1.0, 0.0)


def head_sums(values, ones):
    upper, lower = halves(values)
    return nn(upper, ones) + nn(lower, ones)


def first_half(shape):
    return lax.broadcasted_iota(jnp.int32, shape, len(shape) - 1) < LANES // 2


def both_heads(pair):
    first = first_half((1, LANES))
    mask_a = jnp.where(first, 1.0, 0.0).astype(pair.dtype)
    mask_b = jnp.where(first, 0.0, 1.0).astype(pair.dtype)
    return jnp.concatenate([pair * mask_a, pair * mask_b], 0)


def per_head(stacked):
    rows = stacked.shape[0] // 2
    return jnp.where(first_half((rows, LANES)), stacked[:rows], stacked[rows:])


def compact(full):
    half = LANES // 2
    return jnp.where(first_half((half, LANES)), full[:half], full[half:])


def expand(small, ones):
    return jnp.concatenate([small, small], 0) * ones


def block_state(keys, values):
    return compact(tn(keys, values)), jnp.sum(keys.astype(F32), 0, keepdims=True)


def coef_tile(line_ref, pair):
    tiles = []
    for head in range(2):
        row = line_ref[pl.ds(2 * pair + head, 1), :]
        wide = pltpu.roll(
            jnp.broadcast_to(row, (WINDOW, LINE)), LINE - WINDOW + 1, 1, stride=1, stride_axis=0
        )
        tiles.append(wide[:, : 3 * WINDOW])
    return jnp.concatenate(tiles, 0)


def far_coefs(line_ref, pair):
    first = first_half((1, LANES))
    row_a = line_ref[pl.ds(2 * pair, 1), :]
    row_b = line_ref[pl.ds(2 * pair + 1, 1), :]
    left = jnp.where(first, row_a[:, 0:1], row_b[:, 0:1])
    right = jnp.where(first, row_a[:, LINE - 2 : LINE - 1], row_b[:, LINE - 2 : LINE - 1])
    return left, right


def unskew_sum(tile):
    rows = tile.shape[0]
    padded = jnp.concatenate([tile, jnp.zeros((rows, LINE - tile.shape[1]), F32)], 1)
    while rows > 8:
        rows = rows // 2
        padded = pltpu.roll(padded[:rows], rows, 1) + padded[rows:]
    while rows > 1:
        rows = rows // 2
        padded = pltpu.roll(padded[:rows], rows, 1) + padded[rows:]
    return padded


def lanes(pair):
    return pl.ds(pl.multiple_of(pair * LANES, LANES), LANES)


def qkv_phase(x_ref, w_ref, b_ref, omega_ref, q_ref, k_ref, v_ref, qf_ref, kf_ref, head_dim):
    width = x_ref.shape[1]
    x = x_ref[...]
    ones = block_ones(CHUNK, head_dim).astype(BF16)
    factor = head_dim ** (-0.25) / SPREAD
    for part, low_ref, feat_ref in ((1, k_ref, kf_ref), (2, v_ref, None), (0, q_ref, qf_ref)):
        for chunk in range(width // CHUNK):
            cols = slice(chunk * CHUNK, (chunk + 1) * CHUNK)
            wide = slice(part * width + chunk * CHUNK, part * width + (chunk + 1) * CHUNK)
            low = (nn(x, w_ref[:, wide]) + b_ref[:, wide].astype(F32)).astype(BF16)
            low_ref[:, cols] = low
            if feat_ref is not None:
                projected = nn(low, omega_ref[chunk]) * factor
                widened = low.astype(F32)
                half_norm = head_sums(widened * widened, ones) * (0.5 * head_dim ** (-0.5))
                feat_ref[:, cols] = (
                    jnp.exp(projected - half_norm) * head_dim ** (-0.5)
                ).astype(BF16)


def line_phase(bucket_ref, table_ref, line_ref):
    buckets = table_ref.shape[1]
    one_hot = jnp.where(
        lax.broadcasted_iota(jnp.int32, (buckets, LINE), 0) == bucket_ref[...], 1.0, 0.0
    )
    logs = lax.dot_general(
        table_ref[...],
        one_hot,
        (((1,), (0,)), ((), ())),
        precision=lax.Precision.HIGHEST,
        preferred_element_type=F32,
    )
    line_ref[...] = jnp.exp(logs)


def state_phase(kf_ref, v_ref, num_ref, den_ref, total_ref, pairs):
    blocks = kf_ref.shape[0] // WINDOW
    half = LANES // 2

    @pl.loop(0, pairs)
    def _(pair):
        total = jnp.zeros((half, LANES), F32)
        total_den = jnp.zeros((1, LANES), F32)
        for block in range(blocks):
            rows = slice(block * WINDOW, (block + 1) * WINDOW)
            num, den = block_state(kf_ref[rows, lanes(pair)], v_ref[rows, lanes(pair)])
            num_ref[pair * blocks + block] = num
            den_ref[pl.ds(pair * blocks + block, 1), :] = den
            total = total + num
            total_den = total_den + den
        total_ref[pl.ds(pl.multiple_of(pair * half, half), half), :] = total
        total_ref[pl.ds(pairs * half + pair, 1), :] = total_den


def band_forward_phase(
    qf_ref, ke_ref, ve_ref, line_ref, num_ref, den_ref, before_ref, after_ref,
    out_ref, low_ref, denom_ref, left_ref, right_ref, left_den_ref, right_den_ref, pairs, head_dim,
):
    blocks = qf_ref.shape[0] // WINDOW
    half = LANES // 2

    @pl.loop(0, pairs)
    def _(pair):
        ones_f32 = block_ones(LANES, head_dim)
        ones = ones_f32.astype(BF16)
        cols = lanes(pair)
        coef = coef_tile(line_ref, pair)
        left_coef, right_coef = far_coefs(line_ref, pair)
        state_rows = pl.ds(pl.multiple_of(pair * half, half), half)
        den_row = pl.ds(pairs * half + pair, 1)
        edge_low = block_state(ke_ref[:WINDOW, cols], ve_ref[:WINDOW, cols])
        edge_high = block_state(
            ke_ref[(blocks + 1) * WINDOW :, cols], ve_ref[(blocks + 1) * WINDOW :, cols]
        )
        past = (before_ref[state_rows, :], before_ref[den_row, :])
        future = (after_ref[state_rows, :], after_ref[den_row, :])

        def block_of(block):
            index = pair * blocks + block
            return num_ref[index], den_ref[pl.ds(index, 1), :]

        def add(one, two, sign=1.0):
            return tuple(a + sign * b for a, b in zip(one, two))

        lefts = [add(past, edge_low, -1.0), past]
        for block in range(2, blocks):
            lefts.append(add(lefts[-1], block_of(block - 2)))
        rights = [add(future, edge_high, -1.0), future]
        for block in range(2, blocks):
            rights.append(add(rights[-1], block_of(blocks + 1 - block)))
        rights = rights[::-1]
        for block in range(blocks):
            rows = slice(block * WINDOW, (block + 1) * WINDOW)
            window = slice(block * WINDOW, (block + 3) * WINDOW)
            index = pair * blocks + block
            query = qf_ref[rows, cols]
            scores = nt(both_heads(query), ke_ref[window, cols])
            weights = (coef * scores).astype(BF16)
            values = ve_ref[window, cols]
            summed = nn(weights, jnp.concatenate([values, jnp.ones_like(values)], 1))
            numer = per_head(summed[:, :LANES])
            denom = per_head(summed[:, LANES:])
            left, left_den = lefts[block]
            right, right_den = rights[block]
            left_ref[index] = left
            right_ref[index] = right
            left_den_ref[pl.ds(index, 1), :] = left_den
            right_den_ref[pl.ds(index, 1), :] = right_den
            upper, lower = halves(expand(left_coef * left + right_coef * right, ones_f32))
            numer = numer + nn(query, upper) + nn(query, lower)
            den_far = left_coef * left_den + right_coef * right_den
            denom = denom + head_sums(query.astype(F32) * den_far, ones)
            out = numer / denom
            out_ref[rows, cols] = out
            low_ref[rows, cols] = out.astype(BF16)
            denom_ref[rows, cols] = denom


def norm_parts(values):
    center = values - jnp.mean(values, -1, keepdims=True)
    inv_scale = lax.rsqrt(jnp.mean(center * center, -1, keepdims=True) + EPS)
    return center * inv_scale, inv_scale


def out_phase(x_ref, low_ref, w_ref, b_ref, normed_ref, scale_ref):
    first_sum = x_ref[...].astype(F32) + nn(low_ref[...], w_ref[...]) + b_ref[...].astype(F32)
    normed, inv_scale = norm_parts(first_sum)
    normed_ref[...] = normed
    scale_ref[...] = jnp.broadcast_to(inv_scale, scale_ref.shape)


def norm_back(grad_out, normed, inv_scale, gain):
    grad_normed = grad_out * gain
    centered = grad_normed - jnp.mean(grad_normed, -1, keepdims=True)
    return inv_scale * (centered - normed * jnp.mean(grad_normed * normed, -1, keepdims=True))


def ffn_phase(
    normed_ref, scale_ref, gain_one_ref, shift_one_ref, up_ref, b_up_ref, down_ref, b_down_ref,
    gain_two_ref, shift_two_ref, cot_ref, layer_ref, first_ref, low_ref, vec_ref, gup_ref, gdown_ref,
    gbias_ref, act_ref, slope_ref, acc_ref,
):
    shards = up_ref.shape[0]
    normed_one = normed_ref[...]
    hidden_one = normed_one * gain_one_ref[...] + shift_one_ref[...]
    hidden = hidden_one.astype(BF16)
    acc_ref[...] = hidden_one + b_down_ref[...].astype(F32)

    @pl.loop(0, shards)
    def _(shard):
        pre = nn(hidden, up_ref[shard]) + b_up_ref[shard, 0:1, :].astype(F32)
        phi = 0.5 * (1.0 + lax.erf(pre * ROOT_HALF))
        act = (pre * phi).astype(BF16)
        act_ref[shard] = act
        slope_ref[shard] = (phi + pre * INV_ROOT_TAU * jnp.exp(-0.5 * pre * pre)).astype(BF16)
        acc_ref[...] += nt(act, down_ref[shard])

    normed_two, scale_two = norm_parts(acc_ref[...])
    layer_ref[...] = (normed_two * gain_two_ref[...] + shift_two_ref[...]).astype(BF16)
    cot = cot_ref[...].astype(F32)
    grad_second = norm_back(cot, normed_two, scale_two, gain_two_ref[...])
    grad_ffn = grad_second.astype(BF16)
    vec_ref[0:1, :] = jnp.sum(cot * normed_two, 0, keepdims=True)
    vec_ref[1:2, :] = jnp.sum(cot, 0, keepdims=True)
    vec_ref[2:3, :] = jnp.sum(grad_ffn.astype(F32), 0, keepdims=True)
    acc_ref[...] = grad_second
    grad_turned = grad_ffn.T
    hidden_turned = hidden.T

    @pl.loop(0, shards)
    def _(shard):
        grad_act = nn(grad_ffn, down_ref[shard])
        grad_pre = (grad_act * slope_ref[shard].astype(F32)).astype(BF16)
        gdown_ref[shard] = nn(grad_turned, act_ref[shard]).astype(BF16)
        gup_ref[shard] = nn(hidden_turned, grad_pre).astype(BF16)
        gbias_ref[shard] = jnp.broadcast_to(
            jnp.sum(grad_pre.astype(F32), 0, keepdims=True), gbias_ref.shape[1:]
        )
        acc_ref[...] += nt(grad_pre, up_ref[shard])

    grad_hidden = acc_ref[...]
    grad_first = norm_back(grad_hidden, normed_one, scale_ref[:, 0:1], gain_one_ref[...])
    grad_low = grad_first.astype(BF16)
    first_ref[...] = grad_first
    low_ref[...] = grad_low
    vec_ref[3:4, :] = jnp.sum(grad_hidden * normed_one, 0, keepdims=True)
    vec_ref[4:5, :] = jnp.sum(grad_hidden, 0, keepdims=True)
    vec_ref[5:6, :] = jnp.sum(grad_low.astype(F32), 0, keepdims=True)
    vec_ref[6:8, :] = jnp.zeros((2, vec_ref.shape[1]), F32)


def out_back_phase(
    glow_ref, w_ref, low_ref, out_ref, denom_ref, qf_ref, gnum_ref, gden_ref, gw_ref, dnum_ref,
    dden_ref, total_ref, pairs, head_dim,
):
    rows_all = glow_ref.shape[0]
    blocks = rows_all // WINDOW
    half = LANES // 2
    ones = block_ones(LANES, head_dim).astype(BF16)
    grad_low = glow_ref[...]
    gw_ref[...] = tn(low_ref[...], grad_low)
    for pair in range(pairs):
        cols = slice(pair * LANES, (pair + 1) * LANES)
        grad_attn = nt(grad_low, w_ref[cols, :])
        inverse = 1.0 / denom_ref[:, cols]
        grad_num = (grad_attn * inverse).astype(BF16)
        grad_den = -head_sums(grad_num.astype(F32) * out_ref[:, cols], ones)
        gnum_ref[:, cols] = grad_num
        gden_ref[:, cols] = grad_den
        total = jnp.zeros((half, LANES), F32)
        total_den = jnp.zeros((1, LANES), F32)
        for block in range(blocks):
            rows = slice(block * WINDOW, (block + 1) * WINDOW)
            query = qf_ref[rows, cols]
            num = compact(tn(query, grad_num[rows]))
            den = jnp.sum(query.astype(F32) * grad_den[rows], 0, keepdims=True)
            dnum_ref[pair * blocks + block] = num
            dden_ref[pair * blocks + block : pair * blocks + block + 1, :] = den
            total = total + num
            total_den = total_den + den
        total_ref[pair * half : (pair + 1) * half, :] = total
        total_ref[pairs * half + pair : pairs * half + pair + 1, :] = total_den


def row_grads(keys, values, num, den, ones_f32):
    upper, lower = halves(expand(num, ones_f32))
    grad_keys = nt(values, upper) + nt(values, lower) + den
    grad_values = nn(keys, upper) + nn(keys, lower)
    return grad_keys, grad_values


def band_backward_phase(
    qf_ref, ke_ref, ve_ref, line_ref, gnum_ref, gden_ref, dnum_ref, dden_ref, left_ref, right_ref,
    left_den_ref, right_den_ref, gq_ref, gk_ref, gv_ref, gline_ref, coef_grad_ref, pairs, head_dim,
):
    blocks = qf_ref.shape[0] // WINDOW

    @pl.loop(0, pairs)
    def _(pair):
        ones_f32 = block_ones(LANES, head_dim)
        cols = lanes(pair)
        coef = coef_tile(line_ref, pair)
        left_coef, right_coef = far_coefs(line_ref, pair)
        gk_ref[:, cols] = jnp.zeros((gk_ref.shape[0], LANES), F32)
        gv_ref[:, cols] = jnp.zeros((gv_ref.shape[0], LANES), F32)
        coef_grad_ref[...] = jnp.zeros(coef_grad_ref.shape, F32)
        left_sum = jnp.zeros((1, LANES), F32)
        right_sum = jnp.zeros((1, LANES), F32)
        for block in range(blocks):
            rows = slice(block * WINDOW, (block + 1) * WINDOW)
            window = slice(block * WINDOW, (block + 3) * WINDOW)
            index = pair * blocks + block
            query = qf_ref[rows, cols]
            keys = ke_ref[window, cols]
            values = ve_ref[window, cols]
            grad_num = gnum_ref[rows, cols]
            grad_den = gden_ref[rows, cols]
            queries = both_heads(query)
            grads = both_heads(grad_num)
            weights = coef * nt(queries, keys)
            den_column = jnp.concatenate(
                [grad_den[:, 0:1], grad_den[:, LANES // 2 : LANES // 2 + 1]], 0
            )
            grad_weights = nt(grads, values) + den_column
            coef_grad_ref[...] += grad_weights * weights
            grad_scores = (coef * grad_weights).astype(BF16)
            gv_ref[window, cols] += tn(weights.astype(BF16), grads)
            gk_ref[window, cols] += tn(grad_scores, queries)
            grad_query = per_head(nn(grad_scores, keys))
            left, right = left_ref[index], right_ref[index]
            left_den = left_den_ref[pl.ds(index, 1), :]
            right_den = right_den_ref[pl.ds(index, 1), :]
            upper, lower = halves(expand(left_coef * left + right_coef * right, ones_f32))
            den_far = left_coef * left_den + right_coef * right_den
            grad_query = grad_query + nt(grad_num, upper) + nt(grad_num, lower) + grad_den * den_far
            gq_ref[rows, cols] = grad_query
            dnum = dnum_ref[index]
            dden = dden_ref[pl.ds(index, 1), :]
            left_sum = left_sum + jnp.sum(dnum * left, 0, keepdims=True) + dden * left_den
            right_sum = right_sum + jnp.sum(dnum * right, 0, keepdims=True) + dden * right_den
        for edge, block, scale in ((0, 0, left_coef), (blocks + 1, blocks - 1, right_coef)):
            rows = slice(edge * WINDOW, (edge + 1) * WINDOW)
            index = pair * blocks + block
            edge_k, edge_v = row_grads(
                ke_ref[rows, cols],
                ve_ref[rows, cols],
                scale * dnum_ref[index],
                scale * dden_ref[pl.ds(index, 1), :],
                ones_f32,
            )
            gk_ref[rows, cols] -= edge_k
            gv_ref[rows, cols] -= edge_v
        first = first_half((1, LANES))
        positions = lax.broadcasted_iota(jnp.int32, (1, LINE), 1)
        left_all = left_coef * left_sum
        right_all = right_coef * right_sum
        for head in range(2):
            keep = first if head == 0 else jnp.logical_not(first)
            left_one = jnp.sum(jnp.where(keep, left_all, 0.0), 1, keepdims=True)
            right_one = jnp.sum(jnp.where(keep, right_all, 0.0), 1, keepdims=True)
            line = unskew_sum(coef_grad_ref[head * WINDOW : (head + 1) * WINDOW, :])
            line = line + jnp.where(positions == 0, left_one, 0.0)
            line = line + jnp.where(positions == LINE - 2, right_one, 0.0)
            gline_ref[pl.ds(2 * pair + head, 1), :] = line


def key_back_phase(
    kf_ref, v_ref, line_ref, dnum_ref, dden_ref, past_ref, future_ref, low_in_ref, high_in_ref,
    gk_ref, gv_ref, pairs, head_dim,
):
    blocks = kf_ref.shape[0] // WINDOW
    half = LANES // 2

    @pl.loop(0, pairs)
    def _(pair):
        ones_f32 = block_ones(LANES, head_dim)
        cols = lanes(pair)
        left_coef, right_coef = far_coefs(line_ref, pair)
        state_rows = pl.ds(pl.multiple_of(pair * half, half), half)
        den_row = pl.ds(pairs * half + pair, 1)
        nums = [dnum_ref[pair * blocks + block] for block in range(blocks)]
        dens = [dden_ref[pl.ds(pair * blocks + block, 1), :] for block in range(blocks)]
        for block in range(blocks):
            num_left, den_left = future_ref[state_rows, :], future_ref[den_row, :]
            num_right, den_right = past_ref[state_rows, :], past_ref[den_row, :]
            for other in range(blocks):
                if other >= block + 2:
                    num_left, den_left = num_left + nums[other], den_left + dens[other]
                if other <= block - 2:
                    num_right, den_right = num_right + nums[other], den_right + dens[other]
            rows = slice(block * WINDOW, (block + 1) * WINDOW)
            outer = slice((block + 1) * WINDOW, (block + 2) * WINDOW)
            far_k, far_v = row_grads(
                kf_ref[rows, cols],
                v_ref[rows, cols],
                left_coef * num_left + right_coef * num_right,
                left_coef * den_left + right_coef * den_right,
                ones_f32,
            )
            if block == 0:
                far_k = far_k + low_in_ref[0, :, cols].astype(F32)
                far_v = far_v + low_in_ref[1, :, cols].astype(F32)
            if block == blocks - 1:
                far_k = far_k + high_in_ref[0, :, cols].astype(F32)
                far_v = far_v + high_in_ref[1, :, cols].astype(F32)
            gk_ref[outer, cols] += far_k
            gv_ref[outer, cols] += far_v


def qkv_back_phase(
    x_ref, w_ref, omega_ref, q_ref, k_ref, qf_ref, kf_ref, gq_ref, gk_ref, gv_ref, first_ref,
    gqkv_ref, gtok_ref, gw_ref, gb_ref, head_dim,
):
    rows_all, width = x_ref.shape
    own = slice(WINDOW, WINDOW + rows_all)
    ones = block_ones(CHUNK, head_dim).astype(BF16)
    factor = head_dim ** (-0.25) / SPREAD
    for part, low_ref, feat_ref, grad_ref in (
        (0, q_ref, qf_ref, gq_ref), (1, k_ref, kf_ref, gk_ref), (2, None, None, gv_ref),
    ):
        rows = slice(0, rows_all) if part == 0 else own
        for chunk in range(width // CHUNK):
            cols = slice(chunk * CHUNK, (chunk + 1) * CHUNK)
            wide = slice(part * width + chunk * CHUNK, part * width + (chunk + 1) * CHUNK)
            grad = grad_ref[rows, cols]
            if part < 2:
                inner_up, inner_low = halves(grad * feat_ref[:, cols].astype(F32))
                omega = omega_ref[chunk]
                projected = (nt(inner_up, omega) + nt(inner_low, omega)) * factor
                sums = nn(inner_up, ones) + nn(inner_low, ones)
                grad = projected - sums * head_dim ** (-0.5) * low_ref[:, cols].astype(F32)
            gqkv_ref[:, wide] = grad.astype(BF16)
    gb_ref[...] = jnp.zeros(gb_ref.shape, F32)
    turned = x_ref[...].T
    total = first_ref[...]
    for chunk in range(3 * width // CHUNK):
        wide = slice(chunk * CHUNK, (chunk + 1) * CHUNK)
        grad = gqkv_ref[:, wide]
        gb_ref[0:1, wide] = jnp.sum(grad.astype(F32), 0, keepdims=True)
        gw_ref[:, wide] = nn(turned, grad)
        total = total + nt(grad, w_ref[:, wide])
    gtok_ref[...] = total


def table_phase(gline_ref, bucket_ref, gtable_ref):
    buckets = gtable_ref.shape[1]
    one_hot = jnp.where(
        lax.broadcasted_iota(jnp.int32, (buckets, LINE), 0) == bucket_ref[...], 1.0, 0.0
    )
    gtable_ref[...] = lax.dot_general(
        gline_ref[...],
        one_hot,
        (((1,), (1,)), ((), ())),
        precision=lax.Precision.HIGHEST,
        preferred_element_type=F32,
    )


def call(body, outs, operands, scratch=(), limit=60):
    return pl.pallas_call(
        body,
        out_shape=[jax.ShapeDtypeStruct(shape, dtype) for shape, dtype in outs],
        in_specs=[pl.BlockSpec(memory_space=pltpu.VMEM)] * len(operands),
        out_specs=[pl.BlockSpec(memory_space=pltpu.VMEM)] * len(outs),
        scratch_shapes=list(scratch),
        compiler_params=pltpu.CompilerParams(vmem_limit_bytes=limit * MIB),
    )(*operands)


def shards(
    tokens, cotangent, w_qkv, b_qkv, w_out, b_out, gain_one, shift_one, w_up, b_up, w_down, b_down,
    gain_two, shift_two, feature_codes, bias_table, offset_bucket,
):
    rows, width = tokens.shape[1:]
    heads, head_dim, feats = feature_codes.shape
    buckets = bias_table.shape[1]
    pairs = heads // 2
    blocks = rows // WINDOW
    half = LANES // 2
    hidden_units = w_up.shape[1]
    length = (offset_bucket.shape[0] + 1) // 2
    count = lax.axis_size("seq")
    x = tokens[0]
    omega_int = (feature_codes.astype(F32) - CENTER).astype(BF16)
    group = CHUNK // head_dim
    eye = jnp.eye(group, dtype=BF16)
    omega = (
        omega_int.reshape(heads // group, group, head_dim, 1, feats)
        * eye[None, :, None, :, None]
    ).reshape(heads // group, CHUNK, CHUNK)
    bucket_line = offset_bucket[length - LINE // 2 : length + LINE // 2][None]
    state = (pairs * half + 8, LANES)
    stacked = (pairs * blocks, half, LANES)
    flat = (pairs * blocks, LANES)
    wide = (rows, width)

    def body_one(x_r, w_r, b_r, o_r, bu_r, ta_r, q_r, k_r, v_r, qf_r, kf_r, line_r, num_r, den_r, tot_r):
        qkv_phase(x_r, w_r, b_r, o_r, q_r, k_r, v_r, qf_r, kf_r, head_dim)
        line_phase(bu_r, ta_r, line_r)
        state_phase(kf_r, v_r, num_r, den_r, tot_r, pairs)

    q, k, v, qf, kf, line, num, den, total = call(
        body_one,
        [(wide, BF16)] * 5
        + [((heads, LINE), F32), (stacked, F32), (flat, F32), (state, F32)],
        (x, w_qkv, b_qkv[None], omega, bucket_line, bias_table),
    )
    up_all = lax.all_gather(w_up, "seq", axis=0)
    down_all = lax.all_gather(jnp.transpose(w_down), "seq", axis=0)
    b_up_all = jnp.broadcast_to(lax.all_gather(b_up, "seq", axis=0)[:, None, :], (count, 8, hidden_units))

    def halo(block):
        forward = [(i, i + 1) for i in range(count - 1)]
        backward = [(target, source) for source, target in forward]
        low = lax.ppermute(block[rows - WINDOW :], "seq", forward)
        high = lax.ppermute(block[:WINDOW], "seq", backward)
        return jnp.concatenate([low, block, high], 0)

    me = lax.axis_index("seq")
    ids = jnp.arange(count)

    def prefix(message):
        every = lax.all_gather(message, "seq", axis=0)
        before = jnp.sum(jnp.where((ids < me)[:, None, None], every, 0.0), 0)
        after = jnp.sum(jnp.where((ids > me)[:, None, None], every, 0.0), 0)
        return before, after

    ke, ve = halo(kf), halo(v)
    before, after = prefix(total)

    def body_two(*refs):
        ins, outs = refs[:12], refs[12:]
        qf_r, ke_r, ve_r, line_r, num_r, den_r, bef_r, aft_r, x_r, w_r, b_r, _ = ins
        out_r, low_r, dnm_r, l_r, r_r, ld_r, rd_r, nrm_r, sc_r = outs
        band_forward_phase(
            qf_r, ke_r, ve_r, line_r, num_r, den_r, bef_r, aft_r,
            out_r, low_r, dnm_r, l_r, r_r, ld_r, rd_r, pairs, head_dim,
        )
        out_phase(x_r, low_r, w_r, b_r, nrm_r, sc_r)

    attn, attn_low, denom, left, right, left_den, right_den, normed, scale = call(
        body_two,
        [(wide, F32), (wide, BF16), (wide, F32), (stacked, F32), (stacked, F32), (flat, F32),
         (flat, F32), (wide, F32), ((rows, LANES), F32)],
        (qf, ke, ve, line, num, den, before, after, x, w_out, b_out[None], gain_one[None]),
    )
    layer, first, first_low, vec, gup, gdown, gbias = call(
        ffn_phase,
        [(wide, BF16), (wide, F32), (wide, BF16), ((8, width), F32),
         ((count, width, hidden_units), BF16), ((count, width, hidden_units), BF16),
         ((count, 8, hidden_units), F32)],
        (normed, scale, gain_one[None], shift_one[None], up_all, b_up_all, down_all, b_down[None],
         gain_two[None], shift_two[None], cotangent[0]),
        (pltpu.VMEM((count, rows, hidden_units), BF16), pltpu.VMEM((count, rows, hidden_units), BF16),
         pltpu.VMEM(wide, F32)),
    )

    def reduced(part):
        return lax.psum(lax.psum_scatter(part, "seq", scatter_dimension=0), "row").astype(F32)

    grad_w_up = reduced(gup)
    grad_w_down = jnp.transpose(reduced(gdown))
    grad_b_up = reduced(gbias[:, 0])
    ext = (rows + 2 * WINDOW, width)

    def body_four(*refs):
        (gl_r, w_r, lo_r, ou_r, dn_r, qf_r, ke_r, ve_r, li_r, l_r, r_r, ld_r, rd_r, bu_r) = refs[:14]
        gw_r, gq_r, gk_r, gv_r, dnum_r, dden_r, tot_r, gt_r, gnum_r, gden_r, gline_r, cg_r = refs[14:]
        out_back_phase(
            gl_r, w_r, lo_r, ou_r, dn_r, qf_r, gnum_r, gden_r, gw_r, dnum_r, dden_r, tot_r, pairs, head_dim
        )
        band_backward_phase(
            qf_r, ke_r, ve_r, li_r, gnum_r, gden_r, dnum_r, dden_r, l_r, r_r, ld_r, rd_r,
            gq_r, gk_r, gv_r, gline_r, cg_r, pairs, head_dim,
        )
        table_phase(gline_r, bu_r, gt_r)

    gw_out, gq, gk, gv, dnum, dden, gtotal, gtable = call(
        body_four,
        [((width, width), F32), (wide, F32), (ext, F32), (ext, F32), (stacked, F32), (flat, F32),
         (state, F32), (bias_table.shape, F32)],
        (first_low, w_out, attn_low, attn, denom, qf, ke, ve, line, left, right, left_den, right_den,
         bucket_line),
        (pltpu.VMEM(wide, BF16), pltpu.VMEM(wide, F32), pltpu.VMEM((heads, LINE), F32),
         pltpu.VMEM((2 * WINDOW, 3 * WINDOW), F32)),
    )
    past, future = prefix(gtotal)
    forward = [(i, i + 1) for i in range(count - 1)]
    backward = [(target, source) for source, target in forward]
    to_left = jnp.stack([gk[:WINDOW], gv[:WINDOW]]).astype(BF16)
    to_right = jnp.stack([gk[rows + WINDOW :], gv[rows + WINDOW :]]).astype(BF16)
    low_in = lax.ppermute(to_right, "seq", forward)
    high_in = lax.ppermute(to_left, "seq", backward)

    def body_five(*refs):
        (x_r, w_r, o_r, q_r, k_r, v_r, qf_r, kf_r, li_r, dn_r, dd_r, pa_r, fu_r, lo_r, hi_r, gq_r,
         gki_r, gvi_r, fi_r) = refs[:19]
        gt_r, gw_r, gb_r, gqkv_r, gk_r, gv_r = refs[19:]
        gk_r[...] = gki_r[...]
        gv_r[...] = gvi_r[...]
        key_back_phase(
            kf_r, v_r, li_r, dn_r, dd_r, pa_r, fu_r, lo_r, hi_r, gk_r, gv_r, pairs, head_dim
        )
        qkv_back_phase(
            x_r, w_r, o_r, q_r, k_r, qf_r, kf_r, gq_r, gk_r, gv_r, fi_r, gqkv_r, gt_r, gw_r, gb_r,
            head_dim,
        )

    gtok, gw_qkv, gb_qkv = call(
        body_five,
        [(wide, F32), ((width, 3 * width), F32), ((8, 3 * width), F32)],
        (x, w_qkv, omega, q, k, v, qf, kf, line, dnum, dden, past, future, low_in, high_in, gq, gk, gv,
         first),
        (pltpu.VMEM((rows, 3 * width), BF16), pltpu.VMEM(ext, F32), pltpu.VMEM(ext, F32)),
    )
    summed = lax.psum((gw_qkv, gb_qkv[0], gw_out, vec, gtable), ("row", "seq"))
    gw_qkv, gb_qkv, gw_out, vec, gtable = summed
    return (
        layer[None], gtok[None], gw_qkv, gb_qkv, gw_out, vec[5], vec[3], vec[4], grad_w_up, grad_b_up,
        grad_w_down, vec[2], vec[0], vec[1], gtable,
    )


def solution(mesh):
    placed = (
        P("row", "seq", None), P("row", "seq", None), P(), P(), P(), P(), P(), P(), P(None, "seq"),
        P("seq"), P("seq", None), P(), P(), P(), P(), P(), P(),
    )
    return jax.shard_map(
        shards,
        mesh=mesh,
        in_specs=placed,
        out_specs=(
            P("row", "seq", None), P("row", "seq", None), P(), P(), P(), P(), P(), P(), P(None, "seq"),
            P("seq"), P("seq", None), P(), P(), P(), P(),
        ),
        check_vma=False,
    )
```

time: 1380 us -> 769 us (0.56)
  local copies, waits for them, and re-layouts: 429 us -> 32.9 us
  matrix products: 262 us -> 0 us
  Pallas kernels: 0 us -> 102 us
  other arithmetic: 77.6 us -> 11.7 us
  waiting for transfers between devices: 431 us -> 474 us
  blocking collectives: 147 us -> 114 us
    dot_general x62 -> x0, matrix products: 262 us -> none  [the longest x6 64.7 us: split_left(): jnp.einsum(form, lower, narrow, preferred_element_type=jnp.float32)]
    reshape x4 -> x0, local copies, waits for them, and re-layouts: 233 us -> none  [the longest x1 89.8 us: toeplitz_rows(): flat_line.reshape(head_count, row_count, line_len - 1)[:, :, :col_count]]
    psum x2, waiting for transfers between devices: 0.01 us -> 126 us  [the longest x1 126 us: shards(): summed = lax.psum((gw_qkv, gb_qkv[0], gw_out, vec, gtable), ('row', 'seq'))]
    pallas_call x0 -> x5, Pallas kernels: none -> 102 us  [call(): pl.pallas_call(body, out_shape=[jax.ShapeDtypeStruct(shape, dtype) for sh...]
    reduce_scatter x2, waiting for transfers between devices: 231 us -> 162 us  [reduced(): lax.psum_scatter(part, 'seq', scatter_dimension=0)]
    all_gather x3 -> x1, blocking collectives: 100 us -> 32 us  [shards(): lax.all_gather(b_up, 'seq', axis=0)[:, None, :]]
    another operation x2, local copies, waits for them, and re-layouts: 58.4 us -> 0.06 us  [shards(): to_left = jnp.stack([gk[:WINDOW], gv[:WINDOW]]).astype(BF16)]
    slice x22 -> x6, local copies, waits for them, and re-layouts: 57.5 us -> 5.21 us  [the longest x2 1.47 us: halo(): high = lax.ppermute(block[:WINDOW], 'seq', backward)]
  transfers between devices with their start and end apart: 13 -> 14, of which waited for: 6 -> 6; matrix products, arithmetic and copies ran while one was open for 47% -> 4% of each run, Pallas kernels for 0% -> 8%
where the time goes in v1:
time: 769 us; the launch traced here: 768 us
  waiting for transfers between devices  474 us (62%)
  blocking collectives  114 us (15%)
  Pallas kernels  102 us (13%)
  local copies, waits for them, and re-layouts  32.9 us (4%)
  starting transfers between devices  19.3 us (3%)
  between operations  14.5 us (2%)
  other arithmetic  11.7 us (2%)
    reduce_scatter x2, waiting for transfers between devices, reduced(): lax.psum_scatter(part, 'seq', scatter_dimension=0)  162 us
    psum x1, waiting for transfers between devices, shards(): summed = lax.psum((gw_qkv, gb_qkv[0], gw_out, vec, gtable), ('row', 'seq'))  126 us
    pallas_call x5, Pallas kernels, call(): pl.pallas_call(body, out_shape=[jax.ShapeDtypeStruct(shape, dtype) for sh...  102 us
    all_gather x1, waiting for transfers between devices, shards(): up_all = lax.all_gather(w_up, 'seq', axis=0)  74.2 us
    all_gather x1, waiting for transfers between devices, shards(): down_all = lax.all_gather(jnp.transpose(w_down), 'seq', axis=0)  64.1 us
    all_gather x2, waiting for transfers between devices, prefix(): every = lax.all_gather(message, 'seq', axis=0)  46 us
    psum x1, blocking collectives, shards(): summed = lax.psum((gw_qkv, gb_qkv[0], gw_out, vec, gtable), ('row', 'seq'))  39.6 us
    unnamed x1, blocking collectives  35.1 us
  transfers between devices with their start and end apart: 14, of which 6 were waited for; matrix products, arithmetic and copies ran while one was open for 4% of the time, Pallas kernels for 8%

profile of v1, /device:TPU:0, one launch (start us, length us, event | category | flops | bytes accessed | tf_op | source)
XLA Modules:
  0.0 768.3 jit_solution(17645876959338973534)
XLA Ops:
  7.2 1.0 add_convert_fusion
  9.4 1.3 slice.55
  12.1 9.8 %shard_map.280 = (bf16[512,768]{1,0:T(8,128)(2,1)}, bf16[512,768]{1,0:T(8,128)(2,1)}, bf16[512,768]{1,0:T(8,128)(2,1)}, bf16[512,768]{1,0:T(8,128)(2,1)}, bf16[5...) custom-call(bf16[512,768]{1,0:T(8,128)(2,1)} %bitcast.31, ...), custom_call_target="tpu_custom_call" | custom-call | tf_op jit(solution)/shard_map/pallas_call | solution.py:517
  24.2 4.9 collective-permute-start.2
  29.1 1.3 collective-permute-start.3
  31.2 5.2 collective-permute-start
  36.4 1.3 collective-permute-start.1
  38.9 32.0 %all-gather.5 = bf16[8,1,384]{2,1,0:T(2,128)(2,1)S(1)} all-gather(bf16[1,1,384]{2,1,0:T(2,128)(2,1)S(1)} %reshape.57), channel_id=4, replica_groups=mesh['row'=4,'seq'=8] {'seq'}, dimensions={0}, use_global_device_ids=true | all-gather | bytes 6912 | tf_op jit(solution)/shard_map/all_gather | solution.py:567
  74.3 1.6 constant_dynamic-update-slice_fusion.1
  76.0 2.9 select_reduce_fusion.2
  78.9 12.6 %shard_map.281 = (f32[512,768]{1,0:T(8,128)}, bf16[512,768]{1,0:T(8,128)(2,1)}, f32[512,768]{1,0:T(8,128)}, f32[24,64,128]{2,1,0:T(8,128)}, f32[24,64,128]{2,1,0...) custom-call(bf16[512,768]{1,0:T(8,128)(2,1)} %get-tuple-element.51.refs_0_.refs_5_.r, ...), custom_call_target="tpu_custom_call" | custom-call | tf_op jit(solution)/shard_map/pallas_call | solution.py:517
  91.4 64.1 %all-gather.15.cloned.1.call-done = bf16[6144,384]{0,1:T(8,128)(2,1)} async-done(((bf16[768,384]{0,1:T(8,128)(2,1)}), bf16[6144,384]{0,1:T(8,128)(2,1)}) %all-gather.15.cloned.1.call-update) | async-done | bytes 4718608 | tf_op jit(solution)/shard_map/all_gather | solution.py:566
  155.6 6.6 copy.36
  162.2 74.2 %all-gather.13.cloned.1.call-done = bf16[6144,384]{1,0:T(8,128)(2,1)} async-done(((bf16[768,384]{1,0:T(8,128)(2,1)}), bf16[6144,384]{1,0:T(8,128)(2,1)}) %all-gather.13.cloned.1.call-update) | async-done | bytes 4718608 | tf_op jit(solution)/shard_map/all_gather | solution.py:565
  237.0 34.2 %shard_map.282 = (bf16[512,768]{1,0:T(8,128)(2,1)}, f32[512,768]{1,0:T(8,128)}, bf16[512,768]{1,0:T(8,128)(2,1)}, f32[8,768]{1,0:T(8,128)}, bf16[8,768,384]{2,1,...) custom-call(f32[512,768]{1,0:T(8,128)} %get-tuple-element.58.normed_ref, ...), custom_call_target="tpu_custom_call" | custom-call | tf_op jit(solution)/shard_map/pallas_call | solution.py:517
  272.1 26.6 %shard_map.283 = (f32[768,768]{1,0:T(8,128)}, f32[512,768]{1,0:T(8,128)}, f32[768,768]{1,0:T(8,128)}, f32[768,768]{1,0:T(8,128)}, f32[24,64,128]{2,1,0:T(8,128)}...) custom-call(bf16[512,768]{1,0:T(8,128)(2,1)} %get-tuple-element.63.refs_0_, bf16[768,768]{1,0:T(8,128)(2,1)} %refs_1_.2, ...), custom_call_target="tpu_custom_call" | custom-call | tf_op jit(solution)/shard_map/pallas_call | solution.py:517
  298.8 2.1 convert.17
  301.5 63.3 %reduce-scatter.3.cloned.1.call-done = bf16[1,768,384]{2,1,0:T(8,128)(2,1)} async-done(((bf16[8,768,384]{2,1,0:T(8,128)(2,1)}), bf16[1,768,384]{2,1,0:T(8,128)(2,1)}) %reduce-scatter.3.cloned.1.call-update) | async-done | bytes 589840 | tf_op jit(solution)/shard_map/reduce_scatter | solution.py:616
  364.7 98.5 %reduce-scatter.5.cloned.1.call-done = bf16[1,768,384]{2,1,0:T(8,128)(2,1)} async-done(((bf16[8,768,384]{2,1,0:T(8,128)(2,1)}), bf16[1,768,384]{2,1,0:T(8,128)(2,1)}) %reduce-scatter.5.cloned.1.call-update) | async-done | bytes 589840 | tf_op jit(solution)/shard_map/reduce_scatter | solution.py:616
  463.4 1.3 collective-permute-start.5
  464.7 4.8 collective-permute-start.4
  469.6 46.0 %all-gather.17.cloned.1.call-done = f32[3136,128]{1,0:T(8,128)} async-done(((f32[392,128]{1,0:T(8,128)}), f32[3136,128]{1,0:T(8,128)}) %all-gather.17.cloned.1.call-update) | async-done | bytes 1605648 | tf_op jit(solution)/shard_map/all_gather | solution.py:580
  515.6 2.5 select_reduce_fusion
  519.0 18.7 %shard_map.284 = (f32[512,768]{1,0:T(8,128)}, f32[768,2304]{1,0:T(8,128)}, f32[8,2304]{1,0:T(8,128)}) custom-call(bf16[512,768]{1,0:T(8,128)(2,1)} %bitcast.33, bf16[768,2304]{1,0:T(8,128)(2,1)} %refs_1_.3, bf16[3,256,256]{2,1,0:T(8,128)(2,1)} %broadcast_multiply_fusion.o_r.refs_2_, bf16[512,768]{1,0:T(8,128)(2,1)} %get-tuple-element.61.refs_3_, ...), custom_call_target="tpu_custom_call" | custom-call | tf_op jit(solution)/shard_map/pallas_call | solution.py:517
  539.9 35.1 %all-reduce = f32[8,384]{1,0:T(8,128)S(1)} all-reduce(f32[8,384]{1,0:T(8,128)S(1)} %bitcast.42), channel_id=8, replica_groups=mesh['row'=4,'seq'=8] {'seq'}, use_global_device_ids=true, to_apply=%region_10.11.clone | all-reduce | flops 3072 | bytes 24576
  575.7 6.9 psum.61
  583.5 39.6 %all-reduce.1 = (f32[2304]{0:T(1024)}, f32[8,768]{1,0:T(8,128)S(1)}, f32[12,32]{1,0:T(8,128)}) all-reduce(f32[2304]{0:T(1024)S(1)} %slice_reduce_fusion, f32[8,768]{1,0:T(8,128)S(1)} %copy-done.9, f32[12,32]{1,0:T(8,128)S(1)} %copy-done.10), channel_id=1, replica_groups=mesh['row'=4,'seq'=8] {'row','seq'}, use_global_device_ids=true, to_apply=%region_5.6 | all-reduce | flops 8832 | bytes 70656 | tf_op jit(solution)/shard_map/psum | solution.py:673
  623.8 2.2 convert_element_type.22
  626.0 1.3 copy.37
  627.3 126.2 %all-reduce.7.cloned.1.call-done = (f32[768,2304]{1,0:T(8,128)}, f32[768,768]{1,0:T(8,128)}) async-done(((f32[768,2304]{1,0:T(8,128)}, f32[768,768]{1,0:T(8,128)}), (f32[768,2304]{1,0:T(8,128)}, f32[768,768]{1,0:T(8,128)})) %all-reduce.7.cloned.1.call-update) | async-done | bytes 9437200 | tf_op jit(solution)/shard_map/psum | solution.py:673
  753.5 6.6 copy.52
  760.0 1.4 copy.53
  (99 shorter events, 17.7 us)
Async XLA Ops:
  7.2 68.8 %all-gather.11.cloned.1.call-start = ((), (), s32[]{:S(2)}) async-start(), calls=%async_computation.4 | async-start | bytes 1806336 | tf_op jit(solution)/shard_map/all_gather | solution.py:580
  7.2 3.5 copy-start.11
  21.8 1.7 copy-start.3
  21.8 8.5 %copy-start.4 = (bf16[512,768]{1,0:T(8,128)(2,1)S(1)}, bf16[512,768]{1,0:T(8,128)(2,1)}, u32[]{:S(2)}) copy-start(bf16[512,768]{1,0:T(8,128)(2,1)} %get-tuple-element.52.refs_7_) | copy-start | bytes 2359300
  21.8 15.8 %copy-start.12 = (f32[768]{0:T(1024)S(1)}, f32[768]{0:T(1024)}, u32[]{:S(2)}) copy-start(f32[768]{0:T(1024)} %param.23) | copy-start | bytes 9220
  21.9 16.4 %copy-start.16 = (bf16[768]{0:T(1024)(128)(2,1)S(1)}, bf16[768]{0:T(1024)(128)(2,1)}, u32[]{:S(2)}) copy-start(bf16[768]{0:T(1024)(128)(2,1)} %param.22) | copy-start | bytes 4612
  21.9 17.0 %copy-start.18 = (bf16[384]{0:T(512)(128)(2,1)S(1)}, bf16[384]{0:T(512)(128)(2,1)}, u32[]{:S(2)}) copy-start(bf16[384]{0:T(512)(128)(2,1)} %param.26) | copy-start | bytes 2308
  21.9 49.0 %copy-start.13 = (f32[768]{0:T(1024)S(1)}, f32[768]{0:T(1024)}, u32[]{:S(2)}) copy-start(f32[768]{0:T(1024)} %param.24) | copy-start | bytes 9220
  21.9 49.6 %copy-start.17 = (bf16[768]{0:T(1024)(128)(2,1)S(1)}, bf16[768]{0:T(1024)(128)(2,1)}, u32[]{:S(2)}) copy-start(bf16[768]{0:T(1024)(128)(2,1)} %param.28) | copy-start | bytes 4612
  21.9 50.2 %copy-start.14 = (f32[768]{0:T(1024)S(1)}, f32[768]{0:T(1024)}, u32[]{:S(2)}) copy-start(f32[768]{0:T(1024)} %param.29) | copy-start | bytes 9220
  21.9 50.7 %copy-start.15 = (f32[768]{0:T(1024)S(1)}, f32[768]{0:T(1024)}, u32[]{:S(2)}) copy-start(f32[768]{0:T(1024)} %param.30) | copy-start | bytes 9220
  22.0 133.6 %all-gather.15.cloned.1.call-start = ((), (), s32[]{:S(2)}) async-start(), calls=%async_computation.6 | async-start | bytes 5308416 | tf_op jit(solution)/shard_map/all_gather | solution.py:566
  22.7 213.7 %all-gather.13.cloned.1.call-start = ((), (), s32[]{:S(2)}) async-start(), calls=%async_computation.5 | async-start | bytes 5308416 | tf_op jit(solution)/shard_map/all_gather | solution.py:565
  23.4 341.3 %reduce-scatter.3.cloned.1.call-start = ((), (), s32[]{:S(2)}) async-start(), calls=%async_computation.2 | async-start | bytes 5308416 | tf_op jit(solution)/shard_map/reduce_scatter | solution.py:616
  24.2 49.0 %collective-permute-start.2 = (bf16[128,768]{1,0:T(8,128)(2,1)S(1)}, bf16[128,768]{1,0:T(8,128)(2,1)S(1)}, u32[]{:S(2)}, u32[]{:S(2)}) collective-permute-start(bf16[128,768]{1,0:T(8,128)(2,1)S(1)} %get-tuple-element.154), channel_id=1, source_target_pairs={{0,1},{1,2},{2,3},{3,4},{4,5},{5,6},{6,7},{8,9},{9,10},{10,11},{11... | collective-permute-start | bytes 589832 | tf_op jit(solution)/shard_map/ppermute | solution.py:572
  29.1 45.2 %collective-permute-start.3 = (bf16[128,768]{1,0:T(8,128)(2,1)}, bf16[128,768]{1,0:T(8,128)(2,1)S(1)}, u32[]{:S(2)}, u32[]{:S(2)}) collective-permute-start(bf16[128,768]{1,0:T(8,128)(2,1)} %get-tuple-element.153), channel_id=1, source_target_pairs={{1,0},{2,1},{3,2},{4,3},{5,4},{6,5},{7,6},{9,8},{10,9},{11,10},{12... | collective-permute-start | bytes 589832 | tf_op jit(solution)/shard_map/ppermute | solution.py:573
  31.2 42.1 %collective-permute-start = (bf16[128,768]{1,0:T(8,128)(2,1)}, bf16[128,768]{1,0:T(8,128)(2,1)}, u32[]{:S(2)}, u32[]{:S(2)}) collective-permute-start(bf16[128,768]{1,0:T(8,128)(2,1)} %get-tuple-element.156), channel_id=1, source_target_pairs={{0,1},{1,2},{2,3},{3,4},{4,5},{5,6},{6,7},{8,9},{9,10},{10,11},{11... | collective-permute-start | bytes 589832 | tf_op jit(solution)/shard_map/ppermute | solution.py:572
  36.4 39.6 %collective-permute-start.1 = (bf16[128,768]{1,0:T(8,128)(2,1)}, bf16[128,768]{1,0:T(8,128)(2,1)S(1)}, u32[]{:S(2)}, u32[]{:S(2)}) collective-permute-start(bf16[128,768]{1,0:T(8,128)(2,1)} %get-tuple-element.155), channel_id=1, source_target_pairs={{1,0},{2,1},{3,2},{4,3},{5,4},{6,5},{7,6},{9,8},{10,9},{11,10},{12... | collective-permute-start | bytes 589832 | tf_op jit(solution)/shard_map/ppermute | solution.py:573
  74.3 4.6 copy-start.2
  76.0 2.9 copy-start.1
  271.2 192.1 %reduce-scatter.5.cloned.1.call-start = ((), (), s32[]{:S(2)}) async-start(), calls=%async_computation.3 | async-start | bytes 5308416 | tf_op jit(solution)/shard_map/reduce_scatter | solution.py:616
  271.8 243.8 %all-gather.17.cloned.1.call-start = ((), (), s32[]{:S(2)}) async-start(), calls=%async_computation.7 | async-start | bytes 1806336 | tf_op jit(solution)/shard_map/all_gather | solution.py:580
  298.7 325.1 %all-reduce.9.cloned.1.call-start = ((), (), s32[]{:S(2)}) async-start(), calls=%async_computation.9 | async-start | bytes 2359296 | tf_op jit(solution)/shard_map/psum | solution.py:616
  298.8 2.5 copy-start
  463.3 290.1 %all-reduce.7.cloned.1.call-start = ((), (), s32[]{:S(2)}) async-start(), calls=%async_computation.8 | async-start | bytes 18874368 | tf_op jit(solution)/shard_map/psum | solution.py:673
  463.4 54.7 %collective-permute-start.5 = (bf16[2,128,768]{2,1,0:T(8,128)(2,1)S(1)}, bf16[2,128,768]{2,1,0:T(8,128)(2,1)S(1)}, u32[]{:S(2)}, u32[]{:S(2)}) collective-permute-start(bf16[2,128,768]{2,1,0:T(8,128)(2,1)S(1)} %pad_maximum_fusion.1), channel_id=1, source_target_pairs={{1,0},{2,1},{3,2},{4,3},{5,4},{6,5},{7,6},{9,8},{10,9},{11,10},{12... | collective-permute-start | bytes 1179656 | tf_op jit(solution)/shard_map/ppermute | solution.py:650
  464.7 53.4 %collective-permute-start.4 = (bf16[2,128,768]{2,1,0:T(8,128)(2,1)S(1)}, bf16[2,128,768]{2,1,0:T(8,128)(2,1)S(1)}, u32[]{:S(2)}, u32[]{:S(2)}) collective-permute-start(bf16[2,128,768]{2,1,0:T(8,128)(2,1)S(1)} %pad_maximum_fusion), channel_id=1, source_target_pairs={{0,1},{1,2},{2,3},{3,4},{4,5},{5,6},{6,7},{8,9},{9,10},{10,11},{11... | collective-permute-start | bytes 1179656 | tf_op jit(solution)/shard_map/ppermute | solution.py:649
  518.1 0.9 copy-start.8
  537.8 45.8 %copy-start.9 = (f32[8,768]{1,0:T(8,128)S(1)}, f32[8,768]{1,0:T(8,128)}, u32[]{:S(2)}) copy-start(f32[8,768]{1,0:T(8,128)} %get-tuple-element.82) | copy-start | bytes 73732
  537.8 45.8 %copy-start.10 = (f32[12,32]{1,0:T(8,128)S(1)}, f32[12,32]{1,0:T(8,128)}, u32[]{:S(2)}) copy-start(f32[12,32]{1,0:T(8,128)} %get-tuple-element.86) | copy-start | bytes 4612
  623.8 2.2 copy-start.6
  753.5 6.6 copy-start.5
  (2 other events, 1.4 us)
Sparse Core Ops, SparseCore 0:
  22.1 53.0 all-gather.10
  77.3 78.1 all-gather.14
  157.8 78.5 all-gather.12
  271.3 93.3 reduce-scatter.2
  368.2 95.0 reduce-scatter.4
  465.9 49.6 all-gather.16
  518.0 36.2 all-reduce.8
  560.8 192.5 all-reduce.6

commit v2 on v1

--- a/solution.py
+++ b/solution.py
@@ -115,16 +115,16 @@
     return pl.ds(pl.multiple_of(pair * LANES, LANES), LANES)
 
 
-def qkv_phase(x_ref, w_ref, b_ref, omega_ref, q_ref, k_ref, v_ref, qf_ref, kf_ref, head_dim):
+def qkv_phase(x_ref, w_ref, b_ref, omega_ref, parts, head_dim):
     width = x_ref.shape[1]
     x = x_ref[...]
     ones = block_ones(CHUNK, head_dim).astype(BF16)
     factor = head_dim ** (-0.25) / SPREAD
-    for part, low_ref, feat_ref in ((1, k_ref, kf_ref), (2, v_ref, None), (0, q_ref, qf_ref)):
+    for part, low_ref, feat_ref in parts:
         for chunk in range(width // CHUNK):
             cols = slice(chunk * CHUNK, (chunk + 1) * CHUNK)
             wide = slice(part * width + chunk * CHUNK, part * width + (chunk + 1) * CHUNK)
-            low = (nn(x, w_ref[:, wide]) + b_ref[:, wide].astype(F32)).astype(BF16)
+            low = (nn(x, w_ref[:, wide]) + b_ref[part][:, cols]).astype(BF16)
             low_ref[:, cols] = low
             if feat_ref is not None:
                 projected = nn(low, omega_ref[chunk]) * factor
@@ -138,7 +138,7 @@
 def line_phase(bucket_ref, table_ref, line_ref):
     buckets = table_ref.shape[1]
     one_hot = jnp.where(
-        lax.broadcasted_iota(jnp.int32, (buckets, LINE), 0) == bucket_ref[...], 1.0, 0.0
+        lax.broadcasted_iota(jnp.int32, (buckets, LINE), 0) == bucket_ref[...].astype(jnp.int32), 1.0, 0.0
     )
     logs = lax.dot_general(
         table_ref[...],
@@ -169,7 +169,25 @@
         total_ref[pl.ds(pairs * half + pair, 1), :] = total_den
 
 
-def band_forward_phase(
+def band_forward_phase(qf_ref, ke_ref, ve_ref, line_ref, out_ref, denom_ref, first, last):
+    blocks = qf_ref.shape[0] // WINDOW
+
+    @pl.loop(first, last)
+    def _(pair):
+        cols = lanes(pair)
+        coef = coef_tile(line_ref, pair)
+        for block in range(blocks):
+            rows = slice(block * WINDOW, (block + 1) * WINDOW)
+            window = slice(block * WINDOW, (block + 3) * WINDOW)
+            scores = nt(both_heads(qf_ref[rows, cols]), ke_ref[window, cols])
+            weights = (coef * scores).astype(BF16)
+            values = ve_ref[window, cols]
+            summed = nn(weights, jnp.concatenate([values, jnp.ones_like(values)], 1))
+            out_ref[rows, cols] = per_head(summed[:, :LANES])
+            denom_ref[rows, cols] = per_head(summed[:, LANES:])
+
+
+def far_forward_phase(
     qf_ref, ke_ref, ve_ref, line_ref, num_ref, den_ref, before_ref, after_ref,
     out_ref, low_ref, denom_ref, left_ref, right_ref, left_den_ref, right_den_ref, pairs, head_dim,
 ):
@@ -181,7 +199,6 @@
         ones_f32 = block_ones(LANES, head_dim)
         ones = ones_f32.astype(BF16)
         cols = lanes(pair)
-        coef = coef_tile(line_ref, pair)
         left_coef, right_coef = far_coefs(line_ref, pair)
         state_rows = pl.ds(pl.multiple_of(pair * half, half), half)
         den_row = pl.ds(pairs * half + pair, 1)
@@ -208,15 +225,8 @@
         rights = rights[::-1]
         for block in range(blocks):
             rows = slice(block * WINDOW, (block + 1) * WINDOW)
-            window = slice(block * WINDOW, (block + 3) * WINDOW)
             index = pair * blocks + block
             query = qf_ref[rows, cols]
-            scores = nt(both_heads(query), ke_ref[window, cols])
-            weights = (coef * scores).astype(BF16)
-            values = ve_ref[window, cols]
-            summed = nn(weights, jnp.concatenate([values, jnp.ones_like(values)], 1))
-            numer = per_head(summed[:, :LANES])
-            denom = per_head(summed[:, LANES:])
             left, left_den = lefts[block]
             right, right_den = rights[block]
             left_ref[index] = left
@@ -224,9 +234,9 @@
             left_den_ref[pl.ds(index, 1), :] = left_den
             right_den_ref[pl.ds(index, 1), :] = right_den
             upper, lower = halves(expand(left_coef * left + right_coef * right, ones_f32))
-            numer = numer + nn(query, upper) + nn(query, lower)
+            numer = out_ref[rows, cols] + nn(query, upper) + nn(query, lower)
             den_far = left_coef * left_den + right_coef * right_den
-            denom = denom + head_sums(query.astype(F32) * den_far, ones)
+            denom = denom_ref[rows, cols] + head_sums(query.astype(F32) * den_far, ones)
             out = numer / denom
             out_ref[rows, cols] = out
             low_ref[rows, cols] = out.astype(BF16)
@@ -315,7 +325,7 @@
     half = LANES // 2
     ones = block_ones(LANES, head_dim).astype(BF16)
     grad_low = glow_ref[...]
-    gw_ref[...] = tn(low_ref[...], grad_low)
+    gw_ref[...] = tn(low_ref[...], grad_low).astype(gw_ref.dtype)
     for pair in range(pairs):
         cols = slice(pair * LANES, (pair + 1) * LANES)
         grad_attn = nt(grad_low, w_ref[cols, :])
@@ -348,18 +358,19 @@
 
 def band_backward_phase(
     qf_ref, ke_ref, ve_ref, line_ref, gnum_ref, gden_ref, dnum_ref, dden_ref, left_ref, right_ref,
-    left_den_ref, right_den_ref, gq_ref, gk_ref, gv_ref, gline_ref, coef_grad_ref, pairs, head_dim,
+    left_den_ref, right_den_ref, gq_ref, gk_ref, gv_ref, gline_ref, coef_grad_ref, start, stop, first_col, head_dim,
 ):
     blocks = qf_ref.shape[0] // WINDOW
 
-    @pl.loop(0, pairs)
+    @pl.loop(start, stop)
     def _(pair):
         ones_f32 = block_ones(LANES, head_dim)
         cols = lanes(pair)
+        out = lanes(pair - first_col)
         coef = coef_tile(line_ref, pair)
         left_coef, right_coef = far_coefs(line_ref, pair)
-        gk_ref[:, cols] = jnp.zeros((gk_ref.shape[0], LANES), F32)
-        gv_ref[:, cols] = jnp.zeros((gv_ref.shape[0], LANES), F32)
+        gk_ref[:, out] = jnp.zeros((gk_ref.shape[0], LANES), F32)
+        gv_ref[:, out] = jnp.zeros((gv_ref.shape[0], LANES), F32)
         coef_grad_ref[...] = jnp.zeros(coef_grad_ref.shape, F32)
         left_sum = jnp.zeros((1, LANES), F32)
         right_sum = jnp.zeros((1, LANES), F32)
@@ -381,8 +392,8 @@
             grad_weights = nt(grads, values) + den_column
             coef_grad_ref[...] += grad_weights * weights
             grad_scores = (coef * grad_weights).astype(BF16)
-            gv_ref[window, cols] += tn(weights.astype(BF16), grads)
-            gk_ref[window, cols] += tn(grad_scores, queries)
+            gv_ref[window, out] += tn(weights.astype(BF16), grads)
+            gk_ref[window, out] += tn(grad_scores, queries)
             grad_query = per_head(nn(grad_scores, keys))
             left, right = left_ref[index], right_ref[index]
             left_den = left_den_ref[pl.ds(index, 1), :]
@@ -405,8 +416,8 @@
                 scale * dden_ref[pl.ds(index, 1), :],
                 ones_f32,
             )
-            gk_ref[rows, cols] -= edge_k
-            gv_ref[rows, cols] -= edge_v
+            gk_ref[rows, out] -= edge_k
+            gv_ref[rows, out] -= edge_v
         first = first_half((1, LANES))
         positions = lax.broadcasted_iota(jnp.int32, (1, LINE), 1)
         left_all = left_coef * left_sum
@@ -423,12 +434,12 @@
 
 def key_back_phase(
     kf_ref, v_ref, line_ref, dnum_ref, dden_ref, past_ref, future_ref, low_in_ref, high_in_ref,
-    gk_ref, gv_ref, pairs, head_dim,
+    gk_ref, gv_ref, pairs, start, stop, head_dim,
 ):
     blocks = kf_ref.shape[0] // WINDOW
     half = LANES // 2
 
-    @pl.loop(0, pairs)
+    @pl.loop(start, stop)
     def _(pair):
         ones_f32 = block_ones(LANES, head_dim)
         cols = lanes(pair)
@@ -465,46 +476,39 @@
 
 
 def qkv_back_phase(
-    x_ref, w_ref, omega_ref, q_ref, k_ref, qf_ref, kf_ref, gq_ref, gk_ref, gv_ref, first_ref,
-    gqkv_ref, gtok_ref, gw_ref, gb_ref, head_dim,
+    turned_ref, w_ref, omega_ref, q_ref, k_ref, qf_ref, kf_ref, gq_ref, gk_ref, gv_ref, gtok_ref, parts_ref,
+    small_ref, group, head_dim,
 ):
-    rows_all, width = x_ref.shape
+    width, rows_all = turned_ref.shape
     own = slice(WINDOW, WINDOW + rows_all)
     ones = block_ones(CHUNK, head_dim).astype(BF16)
     factor = head_dim ** (-0.25) / SPREAD
-    for part, low_ref, feat_ref, grad_ref in (
-        (0, q_ref, qf_ref, gq_ref), (1, k_ref, kf_ref, gk_ref), (2, None, None, gv_ref),
+    cols = slice(group * CHUNK, (group + 1) * CHUNK)
+    omega = omega_ref[group]
+    lows = []
+    total = gtok_ref[...]
+    for part, low_ref, feat_ref, grad in (
+        (0, q_ref, qf_ref, gq_ref[:, cols]), (1, k_ref, kf_ref, gk_ref[own, cols]), (2, None, None, gv_ref[own, cols]),
     ):
-        rows = slice(0, rows_all) if part == 0 else own
-        for chunk in range(width // CHUNK):
-            cols = slice(chunk * CHUNK, (chunk + 1) * CHUNK)
-            wide = slice(part * width + chunk * CHUNK, part * width + (chunk + 1) * CHUNK)
-            grad = grad_ref[rows, cols]
-            if part < 2:
-                inner_up, inner_low = halves(grad * feat_ref[:, cols].astype(F32))
-                omega = omega_ref[chunk]
-                projected = (nt(inner_up, omega) + nt(inner_low, omega)) * factor
-                sums = nn(inner_up, ones) + nn(inner_low, ones)
-                grad = projected - sums * head_dim ** (-0.5) * low_ref[:, cols].astype(F32)
-            gqkv_ref[:, wide] = grad.astype(BF16)
-    gb_ref[...] = jnp.zeros(gb_ref.shape, F32)
-    turned = x_ref[...].T
-    total = first_ref[...]
-    for chunk in range(3 * width // CHUNK):
-        wide = slice(chunk * CHUNK, (chunk + 1) * CHUNK)
-        grad = gqkv_ref[:, wide]
-        gb_ref[0:1, wide] = jnp.sum(grad.astype(F32), 0, keepdims=True)
-        gw_ref[:, wide] = nn(turned, grad)
-        total = total + nt(grad, w_ref[:, wide])
+        if part < 2:
+            inner_up, inner_low = halves(grad * feat_ref[:, cols].astype(F32))
+            projected = (nt(inner_up, omega) + nt(inner_low, omega)) * factor
+            sums = nn(inner_up, ones) + nn(inner_low, ones)
+            grad = projected - sums * head_dim ** (-0.5) * low_ref[:, cols].astype(F32)
+        low = grad.astype(BF16)
+        lows.append(low)
+        total = total + nt(low, w_ref[:, part * width + group * CHUNK : part * width + (group + 1) * CHUNK])
     gtok_ref[...] = total
-
-
-def table_phase(gline_ref, bucket_ref, gtable_ref):
-    buckets = gtable_ref.shape[1]
+    joined = jnp.concatenate(lows, 1)
+    small_ref[8 + group : 9 + group, :] = jnp.sum(joined.astype(F32), 0, keepdims=True)
+    parts_ref[:, (group + 1) * width : (group + 2) * width] = nn(turned_ref[...], joined).astype(parts_ref.dtype)
+
+
+def table_phase(gline_ref, bucket_ref, buckets):
     one_hot = jnp.where(
-        lax.broadcasted_iota(jnp.int32, (buckets, LINE), 0) == bucket_ref[...], 1.0, 0.0
-    )
-    gtable_ref[...] = lax.dot_general(
+        lax.broadcasted_iota(jnp.int32, (buckets, LINE), 0) == bucket_ref[...].astype(jnp.int32), 1.0, 0.0
+    )
+    return lax.dot_general(
         gline_ref[...],
         one_hot,
         (((1,), (1,)), ((), ())),
@@ -513,15 +517,1138 @@
     )
 
 
-def call(body, outs, operands, scratch=(), limit=60):
+MESH = pl.DeviceIdType.MESH
+
+
+def guarded(when, action):
+    if when is None:
+        action()
+    else:
+        pl.when(when)(action)
+
+
+class Place:
+    def __init__(self, shards):
+        self.row, self.seq = lax.axis_index("row"), lax.axis_index("seq")
+        self.count_b = 2
+        self.count_a = shards // self.count_b
+        self.shards = shards
+        self.x, self.core = self.row // 2, self.row % 2
+        self.a, self.b = self.seq // self.count_b, self.seq % self.count_b
+        self.is_first, self.is_last = self.seq == 0, self.seq == shards - 1
+        self.not_first, self.not_last = self.seq > 0, self.seq < shards - 1
+
+    def at(self, x=None, core=None, a=None, b=None):
+        x = self.x if x is None else x
+        core = self.core if core is None else core
+        a = self.a if a is None else a
+        b = self.b if b is None else b
+        return (x * 2 + core, a * self.count_b + b)
+
+    def beside(self, seq):
+        return (self.row, seq)
+
+    def shard(self, offset):
+        return lax.rem(self.a + offset, self.count_a)
+
+    def nearest(self, step):
+        orders = []
+        for a in range(self.count_a):
+            orders.append(sorted(range(self.count_a), key=lambda other: (abs(other - a), other)))
+        index = jnp.int32(orders[0][step])
+        for a in range(1, self.count_a):
+            index = jnp.where(self.a == a, orders[a][step], index)
+        return index
+
+
+class Sends:
+    def __init__(self):
+        self.started = []
+
+    def send(self, src, dst, send_sem, recv_sem, device, when=None):
+        copy = pltpu.make_async_remote_copy(
+            src_ref=src, dst_ref=dst, send_sem=send_sem, recv_sem=recv_sem, device_id=device,
+            device_id_type=MESH,
+        )
+        guarded(when, copy.start)
+        self.started.append((when, copy))
+
+    def drain(self):
+        for when, copy in self.started:
+            guarded(when, copy.wait_send)
+        self.started = []
+
+
+def arrive(dst, sem, device, when=None):
+    copy = pltpu.make_async_remote_copy(
+        src_ref=dst, dst_ref=dst, send_sem=sem, recv_sem=sem, device_id=device, device_id_type=MESH
+    )
+    guarded(when, copy.wait_recv)
+
+
+class WeightGather:
+    def __init__(self, place, sends, mats, sems):
+        self.place, self.sends, self.mats = place, sends, mats
+        self.z_send, self.z_recv, self.y_send, self.y_recv, self.x_send, self.x_recv, self.c_send, self.c_recv = sems
+        self.third = mats.shape[3] // 3
+
+    def outer(self, a, b, x, core=None):
+        core = self.place.core if core is None else core
+        return self.mats.at[core, a, b, pl.ds(pl.multiple_of(x * 2 * self.third, self.third), self.third), :]
+
+    def middle(self, a, b, core=None):
+        core = self.place.core if core is None else core
+        return self.mats.at[core, a, b, pl.ds(self.third, self.third), :]
+
+    def both(self, a, b, core=None):
+        return ((0, self.outer(a, b, self.place.x, core)), (1, self.middle(a, b, core)))
+
+    def along_a(self, step):
+        p = self.place
+        a = p.nearest(step)
+        for kind, here in self.both(a, p.b):
+            if step > 0:
+                arrive(here, self.z_recv.at[kind, a], p.at())
+            for out, move in ((0, 1), (1, -1)):
+                target = p.a + move
+                ok = jnp.logical_and(target >= 0, target <= p.count_a - 1)
+                if step > 0:
+                    ok = jnp.logical_and(ok, a < p.a if move == 1 else a > p.a)
+                self.sends.send(
+                    here, here, self.z_send.at[out, kind, a], self.z_recv.at[kind, a],
+                    p.at(a=jnp.clip(target, 0, p.count_a - 1)), ok,
+                )
+            self.sends.send(here, here, self.y_send.at[kind, a], self.y_recv.at[kind, a], p.at(b=1 - p.b))
+            if step > 0:
+                self.pass_on(kind, 0, a, here)
+
+    def pass_on(self, kind, column, a, here):
+        p = self.place
+        if kind == 0:
+            self.sends.send(
+                here, here, self.x_send.at[column, a], self.x_recv.at[column, a], p.at(x=1 - p.x)
+            )
+        self.sends.send(
+            here, here, self.c_send.at[kind, column, a], self.c_recv.at[kind, column, a], p.at(core=1 - p.core)
+        )
+
+    def along_b(self, step):
+        p = self.place
+        a = p.nearest(step)
+        for kind, here in self.both(a, 1 - p.b):
+            arrive(here, self.y_recv.at[kind, a], p.at())
+            self.pass_on(kind, 1, a, here)
+
+    def columns(self, step):
+        p = self.place
+        return ((1, 1 - p.b),) if step == 0 else ((0, p.b), (1, 1 - p.b))
+
+    def along_x(self, step):
+        p = self.place
+        a = p.nearest(step)
+        for column, b in self.columns(step):
+            here = self.outer(a, b, 1 - p.x)
+            arrive(here, self.x_recv.at[column, a], p.at())
+            self.sends.send(
+                here, here, self.c_send.at[2, column, a], self.c_recv.at[2, column, a], p.at(core=1 - p.core)
+            )
+
+    def finish(self, step):
+        p = self.place
+        a = p.nearest(step)
+        other = 1 - p.core
+        for column, b in self.columns(step):
+            for kind, here in self.both(a, b, other) + ((2, self.outer(a, b, 1 - p.x, other)),):
+                arrive(here, self.c_recv.at[kind, column, a], p.at())
+
+
+def gather_sems(count_a):
+    dma = pltpu.SemaphoreType.DMA
+    return [
+        dma((2, 2, count_a)), dma((2, count_a)), dma((2, count_a)), dma((2, count_a)),
+        dma((2, count_a)), dma((2, count_a)), dma((3, 2, count_a)), dma((3, 2, count_a)),
+    ]
+
+
+class StateGather:
+    def __init__(self, place, sends, states, sems):
+        self.place, self.sends, self.states = place, sends, states
+        self.z_send, self.z_recv, self.y_send, self.y_recv = sems
+
+    def source(self, offset):
+        p = self.place
+        return lax.rem(p.a + (p.count_a - offset), p.count_a)
+
+    def along_a(self):
+        p = self.place
+        here = self.states.at[p.a, p.b]
+        for offset in range(1, p.count_a):
+            self.sends.send(
+                here, here, self.z_send.at[offset], self.z_recv.at[offset], p.at(a=p.shard(offset))
+            )
+        self.sends.send(here, here, self.y_send.at[0], self.y_recv.at[0], p.at(b=1 - p.b))
+
+    def along_b(self):
+        p = self.place
+        for offset in range(1, p.count_a):
+            here = self.states.at[self.source(offset), p.b]
+            arrive(here, self.z_recv.at[offset], p.at())
+            self.sends.send(here, here, self.y_send.at[offset], self.y_recv.at[offset], p.at(b=1 - p.b))
+
+    def finish(self):
+        p = self.place
+        for offset in range(p.count_a):
+            arrive(self.states.at[self.source(offset), 1 - p.b], self.y_recv.at[offset], p.at())
+
+
+def state_sems(count_a):
+    return [pltpu.SemaphoreType.DMA((count_a,)) for _ in range(4)]
+
+
+def prefix_phase(place, states, before_ref, after_ref):
+    before = jnp.zeros(before_ref.shape, F32)
+    after = jnp.zeros(after_ref.shape, F32)
+    for a in range(place.count_a):
+        for b in range(place.count_b):
+            seq = a * place.count_b + b
+            value = states[a, b].astype(F32)
+            before = before + jnp.where(seq < place.seq, 1.0, 0.0) * value
+            after = after + jnp.where(seq > place.seq, 1.0, 0.0) * value
+    before_ref[...] = before
+    after_ref[...] = after
+
+
+class GradScatter:
+    def __init__(self, place, sends, grads, total, lands, sems):
+        self.place, self.sends, self.grads, self.total = place, sends, grads, total
+        self.core_land, self.stage, self.x_land, self.y_land, self.z_land, self.last_land = lands
+        (self.copy, self.c_send, self.c_recv, self.x_send, self.x_recv, self.y_send, self.y_recv, self.z_send,
+         self.z_recv, self.l_send, self.l_recv) = sems
+        self.third = grads.shape[3] // 3
+
+    def outer(self, x):
+        return pl.ds(pl.multiple_of(x * 2 * self.third, self.third), self.third)
+
+    def window(self):
+        return pl.ds(pl.multiple_of(self.place.x * self.third, self.third), 2 * self.third)
+
+    def start(self, offset):
+        p = self.place
+        a = p.shard(offset)
+        self.sends.send(
+            self.grads.at[1 - p.core, a], self.core_land.at[a], self.c_send.at[offset],
+            self.c_recv.at[offset], p.at(core=1 - p.core),
+        )
+
+    def add(self, ref, land):
+        ref[...] = (ref[...].astype(F32) + land[...].astype(F32)).astype(BF16)
+
+    def staged(self, offset):
+        return pltpu.make_async_copy(
+            self.core_land.at[self.place.shard(offset)], self.stage, self.copy.at[offset]
+        )
+
+    def fetch(self, offset):
+        arrive(self.core_land.at[self.place.shard(offset)], self.c_recv.at[offset], self.place.at())
+        self.staged(offset).start()
+
+    def chip(self, offset):
+        p = self.place
+        a = p.shard(offset)
+        self.staged(offset).wait()
+        self.add(self.grads.at[p.core, a], self.stage)
+        self.sends.send(
+            self.grads.at[p.core, a, :, self.outer(1 - p.x), :], self.x_land.at[a], self.x_send.at[offset],
+            self.x_recv.at[offset], p.at(x=1 - p.x),
+        )
+
+    def along_x(self, offset):
+        p = self.place
+        a = p.shard(offset)
+        arrive(self.x_land.at[a], self.x_recv.at[offset], p.at())
+        self.add(self.grads.at[p.core, a, :, self.outer(p.x), :], self.x_land.at[a])
+        self.sends.send(
+            self.grads.at[p.core, a, 1 - p.b, self.window(), :], self.y_land.at[a], self.y_send.at[offset],
+            self.y_recv.at[offset], p.at(b=1 - p.b),
+        )
+
+    def along_b(self, offset):
+        p = self.place
+        a = p.shard(offset)
+        arrive(self.y_land.at[a], self.y_recv.at[offset], p.at())
+        mine = self.grads.at[p.core, a, p.b, self.window(), :]
+        self.add(mine, self.y_land.at[a])
+        if offset:
+            self.sends.send(
+                mine, self.z_land.at[offset - 1], self.z_send.at[offset], self.z_recv.at[offset], p.at(a=a)
+            )
+
+    def along_a(self):
+        p = self.place
+        own = self.grads.at[p.core, p.a, p.b]
+        mine = own.at[self.window(), :]
+        total = mine[...].astype(F32)
+        for offset in range(1, p.count_a):
+            arrive(self.z_land.at[offset - 1], self.z_recv.at[offset], p.at())
+            total = total + self.z_land[offset - 1].astype(F32)
+        mine[...] = total.astype(BF16)
+        middle = pl.ds(self.third, self.third)
+        outer = self.outer(p.x)
+        self.total[p.core, outer, :] = self.grads[p.core, p.a, p.b, outer, :]
+        self.sends.send(
+            own.at[middle, :], self.last_land, self.l_send.at[0], self.l_recv.at[0], p.at(x=1 - p.x)
+        )
+        here = self.total.at[p.core, outer, :]
+        self.sends.send(here, here, self.l_send.at[1], self.l_recv.at[1], p.at(x=1 - p.x))
+
+    def last_x(self):
+        p = self.place
+        middle = pl.ds(self.third, self.third)
+        arrive(self.last_land, self.l_recv.at[0], p.at())
+        self.total[p.core, middle, :] = (
+            self.grads[p.core, p.a, p.b, middle, :].astype(F32) + self.last_land[...].astype(F32)
+        ).astype(BF16)
+        arrive(self.total.at[p.core, self.outer(1 - p.x), :], self.l_recv.at[1], p.at())
+        here = self.total.at[p.core]
+        self.sends.send(here, here, self.l_send.at[2], self.l_recv.at[2], p.at(core=1 - p.core))
+
+    def finish(self):
+        arrive(self.total.at[1 - self.place.core], self.l_recv.at[2], self.place.at())
+
+
+def scatter_sems(count_a):
+    dma = pltpu.SemaphoreType.DMA
+    return [dma((count_a,)) for _ in range(9)] + [dma((3,)), dma((3,))]
+
+
+class AllReduce:
+    def __init__(self, place, sends, parts, result, lands, done, mixed, sems):
+        self.place, self.sends, self.parts, self.result = place, sends, parts, result
+        self.core_land, self.staged, self.one_land, self.two_land, self.a_land = lands
+        self.done, self.mixed = done, mixed
+        (self.s_send, self.s_recv, self.z_send, self.z_recv, self.g_send, self.g_recv, self.zg_send, self.zg_recv,
+         self.copy) = sems
+        self.half = result.shape[1] // 2
+        self.quarter = self.half // 2
+        self.slim = self.quarter // place.count_a
+
+    def ways(self, index):
+        p = self.place
+        other_x, other_b = p.at(x=1 - p.x), p.at(b=1 - p.b)
+        if index not in self.mixed:
+            return p.x, p.b, other_x, other_b
+        straight = p.core == 0
+        one = tuple(jnp.where(straight, u, w) for u, w in zip(other_x, other_b))
+        two = tuple(jnp.where(straight, w, u) for u, w in zip(other_x, other_b))
+        return jnp.where(straight, p.x, p.b), jnp.where(straight, p.b, p.x), one, two
+
+    def half_rows(self, core):
+        return pl.ds(pl.multiple_of(core * self.half, self.half), self.half)
+
+    def quarter_rows(self, one):
+        start = self.place.core * self.half + one * self.quarter
+        return pl.ds(pl.multiple_of(start, self.quarter), self.quarter)
+
+    def slim_rows(self, one, a):
+        start = self.place.core * self.half + one * self.quarter + a * self.slim
+        return pl.ds(pl.multiple_of(start, self.slim), self.slim)
+
+    def push(self, index):
+        p = self.place
+        blocks = pl.ds(2 * index, 2)
+        self.sends.send(
+            self.parts.at[blocks, self.half_rows(1 - p.core), :], self.core_land.at[blocks],
+            self.s_send.at[0, index], self.s_recv.at[0, index], p.at(core=1 - p.core),
+        )
+
+    def add(self, ref, land):
+        ref[...] = (ref[...].astype(F32) + land[...].astype(F32)).astype(BF16)
+
+    def stage(self, index, number):
+        p = self.place
+        one, two, one_device, two_device = self.ways(index)
+        blocks = pl.ds(2 * index, 2)
+        mine, other = 2 * index + two, 2 * index + 1 - two
+        parts, result = self.parts, self.result
+        if number == 1:
+            land = self.core_land.at[blocks]
+            arrive(land, self.s_recv.at[0, index], p.at())
+            fetch = pltpu.make_async_copy(land, self.staged, self.copy.at[index])
+            fetch.start()
+            fetch.wait()
+            self.add(parts.at[blocks, self.half_rows(p.core), :], self.staged)
+            self.sends.send(
+                parts.at[blocks, self.quarter_rows(1 - one), :], self.one_land.at[blocks],
+                self.s_send.at[1, index], self.s_recv.at[1, index], one_device,
+            )
+        elif number == 2:
+            land = self.one_land.at[blocks]
+            arrive(land, self.s_recv.at[1, index], p.at())
+            self.add(parts.at[blocks, self.quarter_rows(one), :], land)
+            self.sends.send(
+                parts.at[other, self.quarter_rows(one), :], self.two_land.at[index],
+                self.s_send.at[2, index], self.s_recv.at[2, index], two_device,
+            )
+        elif number == 3:
+            land = self.two_land.at[index]
+            arrive(land, self.s_recv.at[2, index], p.at())
+            self.add(parts.at[mine, self.quarter_rows(one), :], land)
+            for offset in range(1, p.count_a):
+                a = p.shard(offset)
+                self.sends.send(
+                    parts.at[mine, self.slim_rows(one, a), :], self.a_land.at[index, offset - 1],
+                    self.z_send.at[index, offset], self.z_recv.at[index, offset], p.at(a=a),
+                )
+        elif number == 4:
+            rows = self.slim_rows(one, p.a)
+            total = parts[mine, rows, :].astype(F32)
+            for offset in range(1, p.count_a):
+                arrive(self.a_land.at[index, offset - 1], self.z_recv.at[index, offset], p.at())
+                total = total + self.a_land[index, offset - 1].astype(F32)
+            self.done[index] = total.astype(BF16)
+            here = result.at[mine, rows, :]
+            pltpu.make_async_copy(self.done.at[index], here, self.copy.at[index]).start()
+            for offset in range(1, p.count_a):
+                self.sends.send(
+                    self.done.at[index], here, self.zg_send.at[index, offset], self.zg_recv.at[index, offset],
+                    p.at(a=p.shard(offset)),
+                )
+        elif number == 5:
+            pltpu.make_async_copy(
+                self.done.at[index], result.at[mine, self.slim_rows(one, p.a), :], self.copy.at[index]
+            ).wait()
+            for offset in range(1, p.count_a):
+                a = lax.rem(p.a + p.count_a - offset, p.count_a)
+                arrive(result.at[mine, self.slim_rows(one, a), :], self.zg_recv.at[index, offset], p.at())
+            here = result.at[mine, self.quarter_rows(one), :]
+            self.sends.send(here, here, self.g_send.at[0, index], self.g_recv.at[0, index], two_device)
+        elif number == 6:
+            arrive(result.at[other, self.quarter_rows(one), :], self.g_recv.at[0, index], p.at())
+            here = result.at[blocks, self.quarter_rows(one), :]
+            self.sends.send(here, here, self.g_send.at[1, index], self.g_recv.at[1, index], one_device)
+        elif number == 7:
+            arrive(result.at[blocks, self.quarter_rows(1 - one), :], self.g_recv.at[1, index], p.at())
+            here = result.at[blocks, self.half_rows(p.core), :]
+            self.sends.send(here, here, self.g_send.at[2, index], self.g_recv.at[2, index], p.at(core=1 - p.core))
+        elif number == 8:
+            arrive(result.at[blocks, self.half_rows(1 - p.core), :], self.g_recv.at[2, index], p.at())
+
+
+def reduce_sems(chunks, count_a):
+    dma = pltpu.SemaphoreType.DMA
+    return [
+        dma((3, chunks)), dma((3, chunks)), dma((chunks, count_a)), dma((chunks, count_a)),
+        dma((3, chunks)), dma((3, chunks)), dma((chunks, count_a)), dma((chunks, count_a)), dma((chunks,)),
+    ]
+
+
+class SmallReduce:
+    def __init__(self, place, sends, held, land, sems):
+        self.place, self.sends, self.held, self.land = place, sends, held, land
+        self.out_sem, self.in_sem = sems
+        p = place
+        self.devices = [p.at(core=1 - p.core), p.at(x=1 - p.x), p.at(b=1 - p.b)]
+
+    def send(self, step):
+        if step < 3:
+            self.sends.send(
+                self.held.at[step], self.land.at[step], self.out_sem.at[step], self.in_sem.at[step],
+                self.devices[step],
+            )
+            return
+        p = self.place
+        for offset in range(1, p.count_a):
+            self.sends.send(
+                self.held.at[3], self.land.at[3 + offset], self.out_sem.at[3 + offset],
+                self.in_sem.at[3 + offset], p.at(a=p.shard(offset)),
+            )
+
+    def receive(self, step):
+        p = self.place
+        if step < 3:
+            arrive(self.land.at[step], self.in_sem.at[step], p.at())
+            self.held[step + 1] = self.held[step] + self.land[step]
+            return
+        for offset in range(1, p.count_a):
+            arrive(self.land.at[3 + offset], self.in_sem.at[3 + offset], p.at())
+        self.land[3] = self.held[3]
+
+    def total(self):
+        p = self.place
+        total = self.land[3 + lax.rem(p.a, p.count_a)]
+        for a in range(1, p.count_a):
+            total = total + self.land[3 + lax.rem(p.a + p.count_a - a, p.count_a)]
+        return total
+
+
+def halo_phase(x_ref, w_ref, b_ref, omega_ref, k_ref, kv_ref, place, head_dim):
+    rows_ext, width = x_ref.shape
+    low, high = slice(0, WINDOW), slice(rows_ext - WINDOW, rows_ext)
+    x = jnp.concatenate([x_ref[low, :], x_ref[high, :]], 0)
+    ones = block_ones(CHUNK, head_dim).astype(BF16)
+    factor = head_dim ** (-0.25) / SPREAD
+    row = lax.broadcasted_iota(jnp.int32, (2 * WINDOW, 1), 0)
+    inside = jnp.logical_or(
+        jnp.logical_and(row < WINDOW, place.seq > 0),
+        jnp.logical_and(row >= WINDOW, place.seq < place.shards - 1),
+    )
+    for part in (1, 2):
+        for chunk in range(width // CHUNK):
+            cols = slice(chunk * CHUNK, (chunk + 1) * CHUNK)
+            wide = slice(part * width + chunk * CHUNK, part * width + (chunk + 1) * CHUNK)
+            value = (nn(x, w_ref[:, wide]) + b_ref[part][:, cols]).astype(BF16)
+            if part == 1:
+                k_ref[low, cols], k_ref[high, cols] = value[:WINDOW], value[WINDOW:]
+                widened = value.astype(F32)
+                half_norm = head_sums(widened * widened, ones) * (0.5 * head_dim ** (-0.5))
+                value = jnp.exp(nn(value, omega_ref[chunk]) * factor - half_norm) * head_dim ** (-0.5)
+            value = jnp.where(inside, value.astype(F32), 0.0).astype(BF16)
+            kv_ref[part - 1, low, cols], kv_ref[part - 1, high, cols] = value[:WINDOW], value[WINDOW:]
+
+
+def ffn_forward_shard(hidden_ref, mats, a, b, shard, bias_ref, pool, acc_ref):
+    rows = hidden_ref.shape[0]
+    pre = nn(hidden_ref[...], mats[0, a, b]) + bias_ref[shard, 0:1, :]
+    phi = 0.5 * (1.0 + lax.erf(pre * ROOT_HALF))
+    act = (pre * phi).astype(BF16)
+    pool[shard, 0:rows, :] = act
+    pool[shard, rows : 2 * rows, :] = (phi + pre * INV_ROOT_TAU * jnp.exp(-0.5 * pre * pre)).astype(BF16)
+    acc_ref[...] += nt(act, mats[1, a, b])
+
+
+def ffn_backward_shard(grad_ref, grad_turned_ref, hidden_turned_ref, mats, a, b, shard, pool, acc_ref, gbias_ref):
+    rows = grad_ref.shape[0]
+    grad_act = nn(grad_ref[...], mats[1, a, b])
+    grad_pre = (grad_act * pool[shard, rows : 2 * rows, :].astype(F32)).astype(BF16)
+    gbias_ref[shard] = jnp.broadcast_to(
+        jnp.sum(grad_pre.astype(F32), 0, keepdims=True), gbias_ref.shape[1:]
+    )
+    acc_ref[...] += nt(grad_pre, mats[0, a, b])
+    mats[1, a, b] = nn(grad_turned_ref[...], pool[shard, 0:rows, :]).astype(BF16)
+    mats[0, a, b] = nn(hidden_turned_ref[...], grad_pre).astype(BF16)
+
+
+def row_blocks(rows, body, size=CHUNK):
+    @pl.loop(0, rows // size)
+    def _(index):
+        body(pl.ds(pl.multiple_of(index * size, size), size))
+
+
+def hidden_phase(
+    x_ref, low_ref, w_ref, b_ref, gain_ref, shift_ref, b_down_ref, normed_refs, scale_ref, hidden_ref, turned_ref, acc_ref
+):
+    def body(rows):
+        first_sum = x_ref[rows, :].astype(F32) + nn(low_ref[rows, :], w_ref[...]) + b_ref[...].astype(F32)
+        normed, inv_scale = norm_parts(first_sum)
+        normed_refs[0][rows, :], normed_refs[1][rows, :], normed_refs[2][rows, :] = jnp.split(normed, 3, 1)
+        scale_ref[rows, :] = jnp.broadcast_to(inv_scale, (first_sum.shape[0], scale_ref.shape[1]))
+        hidden_one = normed * gain_ref[...] + shift_ref[...]
+        hidden = hidden_one.astype(BF16)
+        hidden_ref[rows, :] = hidden
+        turned_ref[:, rows] = hidden.T
+        acc_ref[rows, :] = hidden_one + b_down_ref[...].astype(F32)
+
+    row_blocks(x_ref.shape[0], body)
+
+
+def middle_phase(acc_ref, cot_ref, gain_two_ref, shift_two_ref, grad_ref, grad_turned_ref, vec_ref):
+    def body(rows):
+        normed_two, scale_two = norm_parts(acc_ref[rows, :])
+        cot = cot_ref[rows, :].astype(F32)
+        cot_ref[rows, :] = (normed_two * gain_two_ref[...] + shift_two_ref[...]).astype(BF16)
+        grad_second = norm_back(cot, normed_two, scale_two, gain_two_ref[...])
+        grad_ffn = grad_second.astype(BF16)
+        vec_ref[0:1, :] += jnp.sum(cot * normed_two, 0, keepdims=True)
+        vec_ref[1:2, :] += jnp.sum(cot, 0, keepdims=True)
+        vec_ref[2:3, :] += jnp.sum(grad_ffn.astype(F32), 0, keepdims=True)
+        acc_ref[rows, :] = grad_second
+        grad_ref[rows, :] = grad_ffn
+        grad_turned_ref[:, rows] = grad_ffn.T
+
+    row_blocks(cot_ref.shape[0], body)
+
+
+def first_back_phase(acc_ref, normed_refs, scale_ref, gain_one_ref, low_ref, vec_ref):
+    def body(rows):
+        grad_hidden = acc_ref[rows, :]
+        normed = jnp.concatenate([ref[rows, :] for ref in normed_refs], 1)
+        grad_first = norm_back(grad_hidden, normed, scale_ref[rows, 0:1], gain_one_ref[...])
+        grad_low = grad_first.astype(BF16)
+        acc_ref[rows, :] = grad_first
+        low_ref[rows, :] = grad_low
+        vec_ref[3:4, :] += jnp.sum(grad_hidden * normed, 0, keepdims=True)
+        vec_ref[4:5, :] += jnp.sum(grad_hidden, 0, keepdims=True)
+        vec_ref[5:6, :] += jnp.sum(grad_low.astype(F32), 0, keepdims=True)
+
+    row_blocks(low_ref.shape[0], body)
+
+
+def attn_back_phase(glow_ref, w_ref, out_ref, denom_ref, low_ref, qf_ref, dnum_ref, dden_ref, total_ref, pairs, head_dim):
+    rows_all = glow_ref.shape[0]
+    blocks = rows_all // WINDOW
+    half = LANES // 2
+    ones = block_ones(LANES, head_dim).astype(BF16)
+    grad_low = glow_ref[...]
+    for pair in range(pairs):
+        cols = slice(pair * LANES, (pair + 1) * LANES)
+        grad_attn = nt(grad_low, w_ref[cols, :])
+        grad_num = (grad_attn / denom_ref[:, cols]).astype(BF16)
+        grad_den = -head_sums(grad_num.astype(F32) * out_ref[:, cols], ones)
+        low_ref[:, cols] = grad_num
+        denom_ref[:, cols] = grad_den
+        total = jnp.zeros((half, LANES), F32)
+        total_den = jnp.zeros((1, LANES), F32)
+        for block in range(blocks):
+            rows = slice(block * WINDOW, (block + 1) * WINDOW)
+            query = qf_ref[rows, cols]
+            num = compact(tn(query, grad_num[rows]))
+            den = jnp.sum(query.astype(F32) * grad_den[rows], 0, keepdims=True)
+            dnum_ref[pair * blocks + block] = num
+            dden_ref[pair * blocks + block : pair * blocks + block + 1, :] = den
+            total = total + num
+            total_den = total_den + den
+        total_ref[pair * half : (pair + 1) * half, :] = total
+        total_ref[pairs * half + pair : pairs * half + pair + 1, :] = total_den
+
+
+def far_back_phase(ke_ref, ve_ref, line_ref, dnum_ref, dden_ref, past_ref, future_ref, gk_ref, gv_ref, pairs, start, stop, first_col, head_dim):
+    blocks = ke_ref.shape[0] // WINDOW - 2
+    half = LANES // 2
+
+    @pl.loop(start, stop)
+    def _(pair):
+        ones_f32 = block_ones(LANES, head_dim)
+        cols = lanes(pair)
+        out = lanes(pair - first_col)
+        left_coef, right_coef = far_coefs(line_ref, pair)
+        state_rows = pl.ds(pl.multiple_of(pair * half, half), half)
+        den_row = pl.ds(pairs * half + pair, 1)
+        nums = [dnum_ref[pair * blocks + block] for block in range(blocks)]
+        dens = [dden_ref[pl.ds(pair * blocks + block, 1), :] for block in range(blocks)]
+        for block in range(blocks):
+            num_left, den_left = future_ref[state_rows, :], future_ref[den_row, :]
+            num_right, den_right = past_ref[state_rows, :], past_ref[den_row, :]
+            for other in range(blocks):
+                if other >= block + 2:
+                    num_left, den_left = num_left + nums[other], den_left + dens[other]
+                if other <= block - 2:
+                    num_right, den_right = num_right + nums[other], den_right + dens[other]
+            rows = slice((block + 1) * WINDOW, (block + 2) * WINDOW)
+            far_k, far_v = row_grads(
+                ke_ref[rows, cols],
+                ve_ref[rows, cols],
+                left_coef * num_left + right_coef * num_right,
+                left_coef * den_left + right_coef * den_right,
+                ones_f32,
+            )
+            gk_ref[rows, out] += far_k
+            gv_ref[rows, out] += far_v
+
+
+def qkv_grad_phase(
+    turned_ref, w_ref, omega_ref, q_ref, k_ref, qf_ref, kf_ref, gq_ref, gk_ref, gv_ref, grads_ref, parts, small_ref,
+    group, place, head_dim,
+):
+    width, rows_ext = turned_ref.shape
+    rows_all = rows_ext - 2 * WINDOW
+    own = slice(WINDOW, WINDOW + rows_all)
+    ones = block_ones(CHUNK, head_dim).astype(BF16)
+    factor = head_dim ** (-0.25) / SPREAD
+    cols = slice(group * CHUNK, (group + 1) * CHUNK)
+    omega = omega_ref[group]
+    base = group * 3 * CHUNK
+    block = parts.shape[2]
+    for part, low_ref, feat_ref in ((0, q_ref, qf_ref), (1, k_ref, kf_ref), (2, None, None)):
+        out = slice(part * CHUNK, (part + 1) * CHUNK)
+
+        def body(rows):
+            if part == 0:
+                grad = gq_ref[rows, cols]
+            else:
+                grad = (gk_ref if part == 1 else gv_ref)[rows, :]
+            if part < 2:
+                inner_up, inner_low = halves(grad * feat_ref[rows, cols].astype(F32))
+                projected = (nt(inner_up, omega) + nt(inner_low, omega)) * factor
+                sums = nn(inner_up, ones) + nn(inner_low, ones)
+                grad = projected - sums * head_dim ** (-0.5) * low_ref[rows, cols].astype(F32)
+            if part > 0:
+                row = lax.broadcasted_iota(jnp.int32, (CHUNK, 1), 0) + rows.start
+                inside = jnp.logical_and(
+                    jnp.logical_or(row >= WINDOW, place.seq > 0),
+                    jnp.logical_or(row < rows_ext - WINDOW, place.seq < place.shards - 1),
+                )
+                grad = jnp.where(inside, grad, 0.0)
+            low = grad.astype(BF16)
+            if part == 0:
+                rows = pl.ds(pl.multiple_of(rows.start + WINDOW, WINDOW), CHUNK)
+            grads_ref[rows, out] = low
+            small_ref[6 + group : 7 + group, out] += jnp.sum(low.astype(F32), 0, keepdims=True)
+
+        row_blocks(rows_all if part == 0 else rows_ext, body)
+        rows = own if part == 0 else slice(0, rows_ext)
+        weight = nn(turned_ref[:, rows], grads_ref[rows, out]).astype(BF16)
+        start = width + base + part * CHUNK
+        done = 0
+        while done < CHUNK:
+            index, at = (start + done) // block, (start + done) % block
+            size = min(CHUNK - done, block - at)
+            parts[index, 0:width, at : at + size] = weight[:, done : done + size]
+            done += size
+
+
+def table_grads(gline_ref, bucket_ref, buckets, small_ref):
+    heads = gline_ref.shape[0]
+    head = lax.broadcasted_iota(jnp.int32, (heads, LANES), 0)
+    lane_bucket = lax.broadcasted_iota(jnp.int32, (LANES, LINE), 0)
+    total = jnp.zeros((heads, LANES), F32)
+    per_row = LANES // buckets
+    for place in range(per_row):
+        one_hot = jnp.where(lane_bucket - place * buckets == bucket_ref[...].astype(jnp.int32), 1.0, 0.0)
+        sums = lax.dot_general(
+            gline_ref[...], one_hot, (((1,), (1,)), ((), ())), precision=lax.Precision.HIGHEST,
+            preferred_element_type=F32,
+        )
+        total = total + jnp.where(head % per_row == place, sums, 0.0)
+    for index in range(heads // per_row):
+        small_ref[13 + index : 14 + index, 0:LANES] = jnp.sum(
+            total[index * per_row : (index + 1) * per_row], 0, keepdims=True
+        )
+
+
+def layer_kernel(pairs, head_dim, buckets, shards, *refs):
+    x_h, cot_h, up_h, down_h, w_r, omega_r, table_r, wo_r, packed_r = refs[:9]
+    layer_h, gtok_h, total_r, small_r, result_h, core_h, ac_h = refs[9:16]
+    (x_r, q_r, k_r, qf_r, kv_r, line_r, num_r, den_r, tot_r, states, states_two, before_r, after_r, left_r, right_r,
+     lden_r, rden_r, attn_r, denom_r, low_r, scale_r, hidden_r, turned_r, cot_r, acc_r,
+     mats, pool, bias_r, gbias_r, gk_r, gv_r, gline_r, cg_r, gqkv_r) = refs[16:50]
+    stage_r, xl_r, yl_r, zl_r, ll_r = refs[50:55]
+    ac_r, ao_r, at_r, aa_r, done_r, held_r, land_r = refs[55:62]
+    sems = refs[62:]
+    all_rows = pl.ds(0, q_r.shape[0])
+    normed_r = (gk_r.at[0, all_rows], gk_r.at[1, all_rows], gv_r.at[0, all_rows])
+    gturned_r = gqkv_r.at[:, all_rows]
+    edge_r, tail_r = cot_r.at[pl.ds(0, 2 * WINDOW)], cot_r.at[pl.ds(2 * WINDOW, 2 * WINDOW)]
+    w_sems, s_sems, s2_sems, rs_sems = sems[:8], sems[8:12], sems[12:16], sems[16:27]
+    ar_sems, sm_sems = sems[27:36], sems[36:38]
+    h_send, h_recv, t_send, t_recv, load_sem = sems[38:]
+    rows, width = q_r.shape
+    half = LANES // 2
+    line = [packed_r.at[pl.ds(index, 1)] for index in range(packed_r.shape[0])]
+    b_r, bo_r, g1_r, s1_r, bdown_r, g2_r, s2_r = line[:3], *line[3:9]
+    bup_r, bucket_r = line[9].at[:, pl.ds(0, up_h.shape[1])], line[10].at[:, pl.ds(0, LINE)]
+    own = pl.ds(WINDOW, rows)
+    place = Place(shards)
+    sends = Sends()
+    seq = place.seq
+    peers = [place.beside(lax.rem(seq + o, shards)) for o in range(1, shards)]
+    peers += [place.at(core=1 - place.core), place.at(x=1 - place.x)]
+    barrier = pltpu.get_barrier_semaphore()
+    for peer in peers:
+        pl.semaphore_signal(barrier, inc=1, device_id=peer, device_id_type=MESH)
+    loads = [
+        pltpu.make_async_copy(src, dst, load_sem.at[i])
+        for i, (src, dst) in enumerate((
+            (down_h, hidden_r.at[pl.ds(0, down_h.shape[0])]), (up_h, mats.at[0, place.a, place.b]),
+            (x_h, x_r.at[own]), (cot_h, cot_r),
+        ))
+    ]
+    for load in loads:
+        load.start()
+    gather = WeightGather(place, sends, mats, w_sems)
+    keys_gather = StateGather(place, sends, states, s_sems)
+    grads_gather = StateGather(place, sends, states_two, s2_sems)
+    scatter = GradScatter(place, sends, mats, total_r, (core_h, stage_r, xl_r, yl_r, zl_r, ll_r), rs_sems)
+    chunks = done_r.shape[0]
+    reduce = AllReduce(place, sends, pool, result_h, (ac_h, ac_r, ao_r, at_r, aa_r), done_r, (chunks - 1,), ar_sems)
+    little = SmallReduce(place, sends, held_r, land_r, sm_sems)
+    to_right = place.beside(jnp.minimum(seq + 1, shards - 1))
+    to_left = place.beside(jnp.maximum(seq - 1, 0))
+    low_edge, high_edge = pl.ds(0, WINDOW), pl.ds(rows + WINDOW, WINDOW)
+
+    small_r[...] = jnp.zeros(small_r.shape, F32)
+    acc_r[0:WINDOW, :] = jnp.zeros((WINDOW, width), F32)
+    acc_r[rows + WINDOW :, :] = jnp.zeros((WINDOW, width), F32)
+    loads[0].wait()
+    mats[1, place.a, place.b] = hidden_r[0 : down_h.shape[0], :].T
+    loads[1].wait()
+    loads[2].wait()
+    pl.semaphore_wait(barrier, len(peers))
+    sends.send(
+        x_r.at[pl.ds(rows, WINDOW)], x_r.at[low_edge], h_send.at[0], h_recv.at[0], to_right, place.not_last
+    )
+    sends.send(
+        x_r.at[pl.ds(WINDOW, WINDOW)], x_r.at[high_edge], h_send.at[1], h_recv.at[1], to_left, place.not_first
+    )
+    gather.along_a(0)
+
+    @pl.when(place.is_first)
+    def _():
+        x_r[0:WINDOW, :] = jnp.zeros((WINDOW, width), BF16)
+
+    @pl.when(place.is_last)
+    def _():
+        x_r[rows + WINDOW :, :] = jnp.zeros((WINDOW, width), BF16)
+
+    ke_r, ve_r = kv_r.at[0], kv_r.at[1]
+    qkv_phase(
+        x_r.at[own], w_r, b_r, omega_r, ((1, k_r.at[own], ke_r.at[own]), (2, ve_r.at[own], None)), head_dim
+    )
+    tot_r[pairs * half :, :] = jnp.zeros((tot_r.shape[0] - pairs * half, LANES), F32)
+    state_phase(ke_r.at[own], ve_r.at[own], num_r, den_r, tot_r, pairs)
+    bias_rows = bup_r.shape[1] // LANES
+    for index in range(bias_rows):
+        at = pairs * (half + 1) + index
+        tot_r[at : at + 1, :] = bup_r[:, index * LANES : (index + 1) * LANES].astype(F32)
+    states[place.a, place.b] = tot_r[...].astype(BF16)
+    keys_gather.along_a()
+    gather.along_b(0)
+    qkv_phase(x_r.at[own], w_r, b_r, omega_r, ((0, q_r, qf_r),), head_dim)
+    gather.along_a(1)
+    line_phase(bucket_r, table_r, line_r)
+    arrive(x_r.at[low_edge], h_recv.at[0], place.at(), place.not_first)
+    arrive(x_r.at[high_edge], h_recv.at[1], place.at(), place.not_last)
+    halo_phase(x_r, w_r, b_r, omega_r, k_r, kv_r, place, head_dim)
+    gather.along_x(0)
+    keys_gather.along_b()
+    third = pairs // 3
+    band_forward_phase(qf_r, ke_r, ve_r, line_r, attn_r, denom_r, 0, third)
+    gather.along_b(1)
+    gather.along_a(2)
+    band_forward_phase(qf_r, ke_r, ve_r, line_r, attn_r, denom_r, third, 2 * third)
+    gather.along_x(1)
+    band_forward_phase(qf_r, ke_r, ve_r, line_r, attn_r, denom_r, 2 * third, pairs)
+    gather.along_b(2)
+    keys_gather.finish()
+    prefix_phase(place, states, before_r, after_r)
+    for a in range(place.count_a):
+        for b in range(place.count_b):
+            tail = states[a, b, pairs * half :, :].astype(F32)
+            bias_r[a * place.count_b + b] = jnp.broadcast_to(
+                jnp.concatenate([tail[pairs + i : pairs + i + 1] for i in range(bias_rows)], 1), bias_r.shape[1:]
+            )
+    far_forward_phase(
+        qf_r, ke_r, ve_r, line_r, num_r, den_r, before_r, after_r, attn_r, low_r, denom_r, left_r, right_r, lden_r,
+        rden_r, pairs, head_dim,
+    )
+    gather.along_a(3)
+    gather.along_x(2)
+    hidden_turned = turned_r.at[:, pl.ds(0, rows)]
+    acc = acc_r.at[own]
+    hidden_phase(
+        x_r.at[own], low_r, wo_r, bo_r, g1_r, s1_r, bdown_r, normed_r, scale_r, hidden_r, hidden_turned, acc
+    )
+
+    def ffn(step, forward):
+        a = place.nearest(step) if forward else place.shard(step)
+
+        @pl.loop(0, place.count_b)
+        def _(index):
+            b = lax.rem(place.b + index, place.count_b)
+            shard = a * place.count_b + b
+            if forward:
+                ffn_forward_shard(hidden_r, mats, a, b, shard, bias_r, pool, acc)
+            else:
+                ffn_backward_shard(hidden_r, gturned_r, hidden_turned, mats, a, b, shard, pool, acc, gbias_r)
+
+    gather.finish(0)
+    ffn(0, True)
+    gather.along_b(3)
+    gather.finish(1)
+    ffn(1, True)
+    gather.along_x(3)
+    gather.finish(2)
+    ffn(2, True)
+    gather.finish(3)
+    ffn(3, True)
+    sends.drain()
+    loads[3].wait()
+    middle_phase(acc, cot_r, g2_r, s2_r, hidden_r, gturned_r, small_r)
+    layer_out = pltpu.make_async_copy(cot_r, layer_h, load_sem.at[4])
+    layer_out.start()
+    ffn(1, False)
+    scatter.start(1)
+    ffn(2, False)
+    scatter.start(2)
+    scatter.fetch(1)
+    ffn(3, False)
+    scatter.start(3)
+    scatter.chip(1)
+    scatter.fetch(2)
+    ffn(0, False)
+    scatter.start(0)
+    scatter.chip(2)
+    scatter.along_x(1)
+    scatter.fetch(3)
+    first_back_phase(acc, normed_r, scale_r, g1_r, hidden_r, small_r)
+    tot_r[pairs * half :, :] = jnp.zeros((tot_r.shape[0] - pairs * half, LANES), F32)
+    block = pool.shape[2]
+    for index in range(width // block):
+        cols = slice(index * block, (index + 1) * block)
+        pool[index, 0:width, :] = tn(low_r[...], hidden_r[:, cols]).astype(BF16)
+    reduce.push(0)
+    attn_back_phase(hidden_r, wo_r, attn_r, denom_r, low_r, qf_r, num_r, den_r, tot_r, pairs, head_dim)
+    layer_out.wait()
+    states_two[place.a, place.b] = tot_r[...].astype(BF16)
+    grads_gather.along_a()
+    scatter.chip(3)
+    scatter.along_x(2)
+    scatter.fetch(0)
+
+    def turn(block):
+        turned_r[:, block] = x_r[block, :].T
+
+    row_blocks(rows + 2 * WINDOW, turn)
+    groups = pairs * LANES // CHUNK
+    in_group = CHUNK // LANES
+
+    def band(group):
+        gk, gv = gk_r.at[group % 2], gv_r.at[group % 2]
+        band_backward_phase(
+            qf_r, ke_r, ve_r, line_r, low_r, denom_r, num_r, den_r, left_r, right_r, lden_r, rden_r, attn_r, gk, gv,
+            gline_r, cg_r, group * in_group, (group + 1) * in_group, group * in_group, head_dim,
+        )
+
+    def keys(group):
+        gk, gv = gk_r.at[group % 2], gv_r.at[group % 2]
+        far_back_phase(
+            ke_r, ve_r, line_r, num_r, den_r, before_r, after_r, gk, gv, pairs, group * in_group,
+            (group + 1) * in_group, group * in_group, head_dim,
+        )
+        qkv_grad_phase(
+            turned_r, w_r, omega_r, q_r, k_r, qf_r, ke_r, attn_r, gk, gv, gqkv_r, pool, small_r, group, place,
+            head_dim,
+        )
+        reduce.push(group + 1)
+
+    def tokens_part(group):
+        def body(block):
+            total = acc_r[block, :]
+            for part in range(3):
+                cols = slice(part * CHUNK, (part + 1) * CHUNK)
+                wide = slice(part * width + group * CHUNK, part * width + (group + 1) * CHUNK)
+                total = total + nt(gqkv_r[block, cols], w_r[:, wide])
+            acc_r[block, :] = total
+
+        row_blocks(rows + 2 * WINDOW, body)
+
+    gqkv_r[0:WINDOW, 0:CHUNK] = jnp.zeros((WINDOW, CHUNK), BF16)
+    gqkv_r[rows + WINDOW :, 0:CHUNK] = jnp.zeros((WINDOW, CHUNK), BF16)
+    band(0)
+    scatter.along_b(1)
+    scatter.chip(0)
+    scatter.along_x(3)
+    reduce.stage(0, 1)
+    grads_gather.along_b()
+    band(1)
+    scatter.along_b(2)
+    scatter.along_x(0)
+    reduce.stage(0, 2)
+    grads_gather.finish()
+    prefix_phase(place, states_two, before_r, after_r)
+    keys(0)
+    scatter.along_b(3)
+    reduce.stage(0, 3)
+    reduce.stage(1, 1)
+    tokens_part(0)
+    band(2)
+    scatter.along_b(0)
+    reduce.stage(0, 4)
+    reduce.stage(1, 2)
+    keys(1)
+    reduce.stage(0, 5)
+    reduce.stage(1, 3)
+    reduce.stage(2, 1)
+    tokens_part(1)
+    keys(2)
+    scatter.along_a()
+    table_grads(gline_r, bucket_r, buckets, small_r)
+    per_row = width // gbias_r.shape[2]
+    for index in range(shards // per_row):
+        small_r[9 + index : 10 + index, :] = jnp.concatenate(
+            [gbias_r[index * per_row + i, 0:1, :] for i in range(per_row)], 1
+        )
+    held_r[0] = small_r[...]
+    little.send(0)
+    reduce.stage(3, 1)
+    reduce.stage(0, 6)
+    reduce.stage(1, 4)
+    reduce.stage(2, 2)
+    little.receive(0)
+    little.send(1)
+
+    reduce.stage(3, 2)
+    reduce.stage(2, 3)
+    reduce.stage(1, 5)
+    reduce.stage(0, 7)
+    scatter.last_x()
+    little.receive(1)
+    little.send(2)
+    reduce.stage(3, 3)
+    reduce.stage(2, 4)
+    reduce.stage(1, 6)
+    tokens_part(2)
+    edge_r[0:WINDOW, :] = acc_r[0:WINDOW, :].astype(BF16)
+    edge_r[WINDOW:, :] = acc_r[rows + WINDOW :, :].astype(BF16)
+    top, bottom = pl.ds(0, WINDOW), pl.ds(WINDOW, WINDOW)
+    sends.send(edge_r.at[top], tail_r.at[bottom], t_send.at[0], t_recv.at[1], to_left, place.not_first)
+    sends.send(edge_r.at[bottom], tail_r.at[top], t_send.at[1], t_recv.at[0], to_right, place.not_last)
+    reduce.stage(3, 4)
+    reduce.stage(2, 5)
+    reduce.stage(1, 7)
+    little.receive(2)
+    little.send(3)
+    reduce.stage(3, 5)
+    reduce.stage(2, 6)
+    arrive(tail_r.at[top], t_recv.at[0], place.at(), place.not_first)
+    arrive(tail_r.at[bottom], t_recv.at[1], place.at(), place.not_last)
+
+    @pl.when(place.not_first)
+    def _():
+        acc_r[WINDOW : 2 * WINDOW, :] += tail_r[0:WINDOW, :].astype(F32)
+
+    @pl.when(place.not_last)
+    def _():
+        acc_r[rows : rows + WINDOW, :] += tail_r[WINDOW:, :].astype(F32)
+
+    tokens_out = pltpu.make_async_copy(acc, gtok_h, load_sem.at[5])
+    tokens_out.start()
+    reduce.stage(3, 6)
+    reduce.stage(2, 7)
+    little.receive(3)
+    small_r[...] = little.total()
+    reduce.stage(3, 7)
+    scatter.finish()
+    for index in range(chunks):
+        reduce.stage(index, 8)
+    tokens_out.wait()
+    sends.drain()
+
+
+def in_parts(grouped):
+    groups = grouped.shape[1] // (3 * CHUNK)
+    starts = [(group * 3 + part) * CHUNK for part in range(3) for group in range(groups)]
+    return jnp.concatenate([grouped[:, start : start + CHUNK].astype(F32) for start in starts], 1)
+
+
+def call(body, outs, operands, scratch=(), limit=60, collective_id=None, in_place=(), out_place=()):
     return pl.pallas_call(
         body,
         out_shape=[jax.ShapeDtypeStruct(shape, dtype) for shape, dtype in outs],
-        in_specs=[pl.BlockSpec(memory_space=pltpu.VMEM)] * len(operands),
-        out_specs=[pl.BlockSpec(memory_space=pltpu.VMEM)] * len(outs),
+        in_specs=[
+            pl.BlockSpec(memory_space=pl.ANY if i in in_place else pltpu.VMEM) for i in range(len(operands))
+        ],
+        out_specs=[
+            pl.BlockSpec(memory_space=pl.ANY if i in out_place else pltpu.VMEM) for i in range(len(outs))
+        ],
         scratch_shapes=list(scratch),
-        compiler_params=pltpu.CompilerParams(vmem_limit_bytes=limit * MIB),
+        compiler_params=pltpu.CompilerParams(
+            vmem_limit_bytes=limit * MIB,
+            collective_id=collective_id,
+            has_side_effects=collective_id is not None,
+        ),
     )(*operands)
+
+
+def unpack_kernel(
+    result_r, total_r, tokens_r, layer_r, small_r, gw_r, gwo_r, gup_r, gdown_r, gtok_r, out_r, gb_r, gbu_r, *vector_rs
+):
+    blocks, width, block = result_r.shape
+    for index in range(blocks):
+        at = 0
+        while at < block:
+            column = index * block + at
+            if column < width:
+                target, place, size = gwo_r, column, block - at
+            else:
+                group, rest = divmod(column - width, 3 * CHUNK)
+                part, inner = divmod(rest, CHUNK)
+                target, place = gw_r, part * width + group * CHUNK + inner
+                size = min(block - at, CHUNK - inner)
+            target[:, place : place + size] = result_r[index, :, at : at + size].astype(F32)
+            at += size
+    gup_r[...] = total_r[0].astype(F32)
+    gdown_r[...] = total_r[1].T.astype(F32)
+    gtok_r[...] = tokens_r[...]
+    out_r[...] = layer_r[...]
+    for index, ref in enumerate(vector_rs):
+        ref[...] = small_r[index, :]
+    for group in range(width // CHUNK):
+        for part in range(3):
+            start = part * width + group * CHUNK
+            gb_r[start : start + CHUNK] = small_r[6 + group, part * CHUNK : (part + 1) * CHUNK]
+    units = gbu_r.shape[0]
+    seq = lax.axis_index("seq")
+    per_row = width // units
+    for shard in range(lax.axis_size("seq")):
+        @pl.when(seq == shard)
+        def _():
+            at = shard % per_row * units
+            gbu_r[...] = small_r[9 + shard // per_row, at : at + units]
+
+
+def fused(
+    x, cot, w_up, w_down, w_qkv, b_qkv, omega, bucket_line, bias_table, w_out, b_out, gain_one, shift_one, b_up, b_down,
+    gain_two, shift_two, pairs, head_dim,
+):
+    rows, width = x.shape
+    units = w_up.shape[1]
+    heads, buckets = bias_table.shape
+    count = lax.axis_size("seq")
+    count_a = count // 2
+    blocks, half = rows // WINDOW, LANES // 2
+    third, quarter = width // 3, width // 4
+    groups = width // CHUNK
+    chunks = 1 + groups
+    columns = chunks * width // units
+    wide, ext = (rows, width), (rows + 2 * WINDOW, width)
+    stacked, flat = (pairs * blocks, half, LANES), (pairs * blocks, LANES)
+    message = (pairs * half + 16, LANES)
+    mats = (2, count_a, 2, width, units)
+    dma = pltpu.SemaphoreType.DMA
+    vmem = pltpu.VMEM
+    vectors = [b_qkv, b_out, gain_one, shift_one, b_down, gain_two, shift_two]
+    vectors += [jnp.pad(vector, (0, width - vector.shape[0])) for vector in (b_up, bucket_line[0])]
+    packed = jnp.concatenate([vector.astype(F32) for vector in vectors]).reshape(-1, width)
+    layer, gtok, total, small, result, _, _ = call(
+        functools.partial(layer_kernel, pairs, head_dim, buckets, count),
+        [(wide, BF16), (wide, F32), ((2, width, units), BF16), ((16, width), F32), ((columns, width, units), BF16),
+         (mats[1:], BF16), ((columns, 2 * quarter, units), BF16)],
+        (x, cot, w_up, w_down, w_qkv, omega, bias_table, w_out, packed),
+        [vmem(ext, BF16), vmem(wide, BF16), vmem(ext, BF16), vmem(wide, BF16), vmem((2, *ext), BF16),
+         vmem((heads, LINE), F32), vmem(stacked, F32), vmem(flat, F32), vmem(message, F32),
+         vmem((count_a, 2, *message), BF16), vmem((count_a, 2, *message), BF16), vmem(message, F32),
+         vmem(message, F32), vmem(stacked, F32), vmem(stacked, F32), vmem(flat, F32), vmem(flat, F32),
+         vmem(wide, F32), vmem(wide, F32), vmem(wide, BF16), vmem((rows, LANES), F32),
+         vmem(wide, BF16), vmem((width, ext[0]), BF16),
+         vmem(wide, BF16), vmem(ext, F32), vmem(mats, BF16), vmem((columns, 2 * rows, units), BF16),
+         vmem((count, 8, units), F32), vmem((count, 8, units), F32), vmem((2, ext[0], CHUNK), F32),
+         vmem((2, ext[0], CHUNK), F32), vmem((heads, LINE), F32), vmem((2 * WINDOW, 3 * WINDOW), F32),
+         vmem(ext, BF16), vmem((2, width, units), BF16), vmem((count_a, 2, third, units), BF16),
+         vmem((count_a, 2 * third, units), BF16), vmem((count_a - 1, 2 * third, units), BF16),
+         vmem((third, units), BF16),
+         vmem((2, 2 * quarter, units), BF16), vmem((columns, quarter, units), BF16),
+         vmem((chunks, quarter, units), BF16), vmem((chunks, count_a - 1, quarter // count_a, units), BF16),
+         vmem((chunks, quarter // count_a, units), BF16), vmem((4, 16, width), F32),
+         vmem((3 + count_a, 16, width), F32)]
+        + gather_sems(count_a) + state_sems(count_a) + state_sems(count_a) + scatter_sems(count_a)
+        + reduce_sems(chunks, count_a)
+        + [dma((3 + count_a,)), dma((3 + count_a,)), dma((2,)), dma((2,)), dma((2,)), dma((2,)), dma((6,))],
+        limit=62,
+        collective_id=0,
+        in_place=(0, 1, 2, 3),
+        out_place=(0, 1, 4, 5, 6),
+    )
+    vector = ((width,), F32)
+    gw_qkv, gw_out, gup, gdown, gtok, layer, gb_qkv, grad_b_up, g2, s2, bd, g1, s1, bo = call(
+        unpack_kernel,
+        [((width, 3 * width), F32), ((width, width), F32), ((width, units), F32), ((units, width), F32), (wide, F32),
+         (wide, BF16), ((3 * width,), F32), ((units,), F32)] + [vector] * 6,
+        (result, total, gtok, layer, small),
+    )
+    gtable = small[13 : 13 + heads * buckets // LANES, :LANES].reshape(heads, buckets)
+    return (
+        layer[None], gtok[None], gw_qkv, gb_qkv, gw_out, bo, g1, s1, gup, grad_b_up, gdown, bd, g2, s2, gtable,
+    )
 
 
 def shards(
@@ -551,21 +1678,6 @@
     flat = (pairs * blocks, LANES)
     wide = (rows, width)
 
-    def body_one(x_r, w_r, b_r, o_r, bu_r, ta_r, q_r, k_r, v_r, qf_r, kf_r, line_r, num_r, den_r, tot_r):
-        qkv_phase(x_r, w_r, b_r, o_r, q_r, k_r, v_r, qf_r, kf_r, head_dim)
-        line_phase(bu_r, ta_r, line_r)
-        state_phase(kf_r, v_r, num_r, den_r, tot_r, pairs)
-
-    q, k, v, qf, kf, line, num, den, total = call(
-        body_one,
-        [(wide, BF16)] * 5
-        + [((heads, LINE), F32), (stacked, F32), (flat, F32), (state, F32)],
-        (x, w_qkv, b_qkv[None], omega, bucket_line, bias_table),
-    )
-    up_all = lax.all_gather(w_up, "seq", axis=0)
-    down_all = lax.all_gather(jnp.transpose(w_down), "seq", axis=0)
-    b_up_all = jnp.broadcast_to(lax.all_gather(b_up, "seq", axis=0)[:, None, :], (count, 8, hidden_units))
-
     def halo(block):
         forward = [(i, i + 1) for i in range(count - 1)]
         backward = [(target, source) for source, target in forward]
@@ -582,6 +1694,28 @@
         after = jnp.sum(jnp.where((ids > me)[:, None, None], every, 0.0), 0)
         return before, after
 
+    if lax.axis_size("row") == 4 and count == 8:
+        return fused(
+            x, cotangent[0], w_up, w_down, w_qkv, b_qkv, omega, bucket_line, bias_table, w_out, b_out, gain_one,
+            shift_one, b_up, b_down, gain_two, shift_two, pairs, head_dim,
+        )
+
+    def body_one(x_r, w_r, b_r, o_r, bu_r, ta_r, q_r, k_r, v_r, qf_r, kf_r, line_r, num_r, den_r, tot_r):
+        parts = ((1, k_r, kf_r), (2, v_r, None), (0, q_r, qf_r))
+        qkv_phase(x_r, w_r, [b_r.at[pl.ds(i, 1)] for i in range(3)], o_r, parts, head_dim)
+        line_phase(bu_r, ta_r, line_r)
+        state_phase(kf_r, v_r, num_r, den_r, tot_r, pairs)
+
+    q, k, v, qf, kf, line, num, den, total = call(
+        body_one,
+        [(wide, BF16)] * 5
+        + [((heads, LINE), F32), (stacked, F32), (flat, F32), (state, F32)],
+        (x, w_qkv, b_qkv.astype(F32).reshape(3, width), omega, bucket_line, bias_table),
+    )
+    up_all = lax.all_gather(w_up, "seq", axis=0)
+    down_all = lax.all_gather(jnp.transpose(w_down), "seq", axis=0)
+    b_up_all = jnp.broadcast_to(lax.all_gather(b_up, "seq", axis=0)[:, None, :], (count, 8, hidden_units))
+
     ke, ve = halo(kf), halo(v)
     before, after = prefix(total)
 
@@ -589,7 +1723,8 @@
         ins, outs = refs[:12], refs[12:]
         qf_r, ke_r, ve_r, line_r, num_r, den_r, bef_r, aft_r, x_r, w_r, b_r, _ = ins
         out_r, low_r, dnm_r, l_r, r_r, ld_r, rd_r, nrm_r, sc_r = outs
-        band_forward_phase(
+        band_forward_phase(qf_r, ke_r, ve_r, line_r, out_r, dnm_r, 0, pairs)
+        far_forward_phase(
             qf_r, ke_r, ve_r, line_r, num_r, den_r, bef_r, aft_r,
             out_r, low_r, dnm_r, l_r, r_r, ld_r, rd_r, pairs, head_dim,
         )
@@ -628,9 +1763,9 @@
         )
         band_backward_phase(
             qf_r, ke_r, ve_r, li_r, gnum_r, gden_r, dnum_r, dden_r, l_r, r_r, ld_r, rd_r,
-            gq_r, gk_r, gv_r, gline_r, cg_r, pairs, head_dim,
-        )
-        table_phase(gline_r, bu_r, gt_r)
+            gq_r, gk_r, gv_r, gline_r, cg_r, 0, pairs, 0, head_dim,
+        )
+        gt_r[...] = table_phase(gline_r, bu_r, buckets)
 
     gw_out, gq, gk, gv, dnum, dden, gtotal, gtable = call(
         body_four,
@@ -652,24 +1787,28 @@
     def body_five(*refs):
         (x_r, w_r, o_r, q_r, k_r, v_r, qf_r, kf_r, li_r, dn_r, dd_r, pa_r, fu_r, lo_r, hi_r, gq_r,
          gki_r, gvi_r, fi_r) = refs[:19]
-        gt_r, gw_r, gb_r, gqkv_r, gk_r, gv_r = refs[19:]
+        gt_r, gw_r, gb_r, gk_r, gv_r, turned_r = refs[19:]
         gk_r[...] = gki_r[...]
         gv_r[...] = gvi_r[...]
+        gt_r[...] = fi_r[...]
+        turned_r[...] = x_r[...].T
         key_back_phase(
-            kf_r, v_r, li_r, dn_r, dd_r, pa_r, fu_r, lo_r, hi_r, gk_r, gv_r, pairs, head_dim
-        )
-        qkv_back_phase(
-            x_r, w_r, o_r, q_r, k_r, qf_r, kf_r, gq_r, gk_r, gv_r, fi_r, gqkv_r, gt_r, gw_r, gb_r,
-            head_dim,
-        )
-
-    gtok, gw_qkv, gb_qkv = call(
+            kf_r, v_r, li_r, dn_r, dd_r, pa_r, fu_r, lo_r, hi_r, gk_r, gv_r, pairs, 0, pairs, head_dim
+        )
+        for group in range(width // CHUNK):
+            qkv_back_phase(
+                turned_r, w_r, o_r, q_r, k_r, qf_r, kf_r, gq_r, gk_r, gv_r, gt_r, gw_r, gb_r, group, head_dim
+            )
+
+    gtok, gw_qkv, small = call(
         body_five,
-        [(wide, F32), ((width, 3 * width), F32), ((8, 3 * width), F32)],
+        [(wide, F32), ((width, 4 * width), F32), ((16, width), F32)],
         (x, w_qkv, omega, q, k, v, qf, kf, line, dnum, dden, past, future, low_in, high_in, gq, gk, gv,
          first),
-        (pltpu.VMEM((rows, 3 * width), BF16), pltpu.VMEM(ext, F32), pltpu.VMEM(ext, F32)),
-    )
+        (pltpu.VMEM(ext, F32), pltpu.VMEM(ext, F32), pltpu.VMEM((width, rows), BF16)),
+    )
+    gw_qkv = in_parts(gw_qkv[:, width:])
+    gb_qkv = in_parts(small[6 : 6 + width // CHUNK].reshape(1, -1))
     summed = lax.psum((gw_qkv, gb_qkv[0], gw_out, vec, gtable), ("row", "seq"))
     gw_qkv, gb_qkv, gw_out, vec, gtable = summed
     return (

time: 769 us -> 244 us (0.32)
  waiting for transfers between devices: 474 us -> 0 us
  Pallas kernels: 102 us -> 233 us
  blocking collectives: 114 us -> 0 us
  local copies, waits for them, and re-layouts: 32.9 us -> 3.85 us
  starting transfers between devices: 19.3 us -> 0 us
  between operations: 14.5 us -> 1.06 us
  other arithmetic: 11.7 us -> 1.9 us
    all_gather x4 -> x0, waiting for transfers between devices: 184 us -> none  [the longest x1 74.2 us: shards(): up_all = lax.all_gather(w_up, 'seq', axis=0)]
    reduce_scatter x2 -> x0, waiting for transfers between devices: 162 us -> none  [reduced(): lax.psum_scatter(part, 'seq', scatter_dimension=0)]
    pallas_call x5 -> x2, Pallas kernels: 102 us -> 233 us  [call(): pl.pallas_call(body, out_shape=[jax.ShapeDtypeStruct(shape, dtype) for sh...]
    psum x2 -> x0, waiting for transfers between devices: 126 us -> none  [the longest x1 126 us: shards(): summed = lax.psum((gw_qkv, gb_qkv[0], gw_out, vec, gtable), ('row', 'seq'))]
    psum x2 -> x0, blocking collectives: 46.5 us -> none  [the longest x1 39.6 us: shards(): summed = lax.psum((gw_qkv, gb_qkv[0], gw_out, vec, gtable), ('row', 'seq'))]
    unnamed x1 -> x0, blocking collectives: 35.1 us -> none
    all_gather x1 -> x0, blocking collectives: 32 us -> none  [shards(): lax.all_gather(b_up, 'seq', axis=0)[:, None, :]]
    ppermute x6 -> x0, starting transfers between devices: 18.8 us -> none  [the longest x2 10.1 us: halo(): low = lax.ppermute(block[rows - WINDOW:], 'seq', forward)]
  transfers between devices with their start and end apart: 14 -> 0, of which waited for: 6 -> 0; matrix products, arithmetic and copies ran while one was open for 4% -> 0% of each run, Pallas kernels for 8% -> 0%
where the time goes in v2:
time: 244 us; the launch traced here: 240 us
  Pallas kernels  233 us (95%)
  local copies, waits for them, and re-layouts  3.85 us (2%)
    pallas_call x2, Pallas kernels, call(): pl.pallas_call(body, out_shape=[jax.ShapeDtypeStruct(shape, dtype) for sh...  233 us

profile of v2, /device:TPU:0, one launch (start us, length us, event | category | flops | bytes accessed | tf_op | source)
XLA Modules:
  0.0 239.6 jit_solution(5708135768949576805)
XLA Ops:
  0.7 0.0 copy-start
  0.7 0.0 copy-start.5
  0.7 0.0 copy-start.1
  0.7 0.0 copy-start.2
  0.7 0.0 copy-start.6
  0.7 0.0 copy-start.3
  0.7 0.0 copy-start.4
  0.7 0.0 copy-start.7
  0.7 1.1 add_convert_fusion
  1.8 0.3 mul.23
  2.1 0.5 mul.24
  2.6 0.1 mul.25
  2.7 0.2 mul.26
  3.0 0.8 broadcast_multiply_fusion.refs_5_
  3.7 0.0 copy-done
  3.8 0.0 copy-done.5
  3.8 0.0 copy-done.1
  3.8 0.0 copy-done.2
  3.8 0.0 copy-done.6
  3.8 0.0 copy-done.3
  3.9 0.0 copy-done.4
  3.9 0.0 copy-done.7
  3.9 0.7 slice.6
  4.6 0.6 reshape.49.refs_8_
  5.3 223.3 %shard_map.280 = (bf16[512,768]{1,0:T(8,128)(2,1)}, f32[512,768]{1,0:T(8,128)}, bf16[2,768,384]{2,1,0:T(8,128)(2,1)}, f32[16,768]{1,0:T(8,128)}, bf16[8,768,384]...) custom-call(bf16[512,768]{1,0:T(8,128)(2,1)} %bitcast.5, bf16[512,768]{1,0:T(8,128)(2,1)} %bitcast.6, ...), custom_call_target="tpu_custom_call" | custom-call | tf_op jit(solution)/shard_map/pallas_call | solution.py:1534
  228.5 9.5 %shard_map.281 = (f32[768,2304]{1,0:T(8,128)}, f32[768,768]{1,0:T(8,128)}, f32[768,384]{1,0:T(8,128)}, f32[384,768]{1,0:T(8,128)}, f32[512,768]{1,0:T(8,128)}, /...) custom-call(bf16[8,768,384]{2,1,0:T(8,128)(2,1)} %get-tuple-element., ...), custom_call_target="tpu_custom_call" | custom-call | tf_op jit(solution)/shard_map/pallas_call | solution.py:1534
  238.0 0.7 slice.7
  238.7 0.7 reshape.50
  (11 shorter events, 0.1 us)
Async XLA Ops:
  0.7 3.1 %copy-start = (bf16[2304]{0:T(1024)(128)(2,1)S(1)}, bf16[2304]{0:T(1024)(128)(2,1)}, u32[]{:S(2)}) copy-start(bf16[2304]{0:T(1024)(128)(2,1)} %param.20) | copy-start | bytes 13828
  0.7 3.1 %copy-start.5 = (bf16[768]{0:T(1024)(128)(2,1)S(1)}, bf16[768]{0:T(1024)(128)(2,1)}, u32[]{:S(2)}) copy-start(bf16[768]{0:T(1024)(128)(2,1)} %param.22) | copy-start | bytes 4612
  0.7 3.1 %copy-start.1 = (f32[768]{0:T(1024)S(1)}, f32[768]{0:T(1024)}, u32[]{:S(2)}) copy-start(f32[768]{0:T(1024)} %param.23) | copy-start | bytes 9220
  0.7 3.1 %copy-start.2 = (f32[768]{0:T(1024)S(1)}, f32[768]{0:T(1024)}, u32[]{:S(2)}) copy-start(f32[768]{0:T(1024)} %param.24) | copy-start | bytes 9220
  0.7 3.1 %copy-start.6 = (bf16[768]{0:T(1024)(128)(2,1)S(1)}, bf16[768]{0:T(1024)(128)(2,1)}, u32[]{:S(2)}) copy-start(bf16[768]{0:T(1024)(128)(2,1)} %param.28) | copy-start | bytes 4612
  0.7 3.1 %copy-start.3 = (f32[768]{0:T(1024)S(1)}, f32[768]{0:T(1024)}, u32[]{:S(2)}) copy-start(f32[768]{0:T(1024)} %param.29) | copy-start | bytes 9220
  0.7 3.2 %copy-start.4 = (f32[768]{0:T(1024)S(1)}, f32[768]{0:T(1024)}, u32[]{:S(2)}) copy-start(f32[768]{0:T(1024)} %param.30) | copy-start | bytes 9220
  0.7 3.2 %copy-start.7 = (bf16[384]{0:T(512)(128)(2,1)S(1)}, bf16[384]{0:T(512)(128)(2,1)}, u32[]{:S(2)}) copy-start(bf16[384]{0:T(512)(128)(2,1)} %param.26) | copy-start | bytes 2308
